TPU v7x, 128 devices: a whole 4x4x4 slice. The times are simulated.
128 devices in a mesh: section: 2 (over core), dp: 8 (over x_hi, z), mp: 8 (over x_lo, y).
Axes of the slice: x: 4 (x_hi: 2, x_lo: 2; x = x_hi * 2 + x_lo), y: 4, z: 4, core: 2. Of those that a mesh axis runs over, the one named last changes fastest.
Arguments:
- fwd_in: bfloat16 [2, 8, 8, 256, 1536], P('section', 'dp', 'mp'), may hold values from -6 to 6
- kept_in: bfloat16 [2, 8, 8, 256, 1536], P('section', 'dp', 'mp'), may hold values from -6 to 6
- cotangent: bfloat16 [2, 8, 8, 256, 1536], P('section', 'dp', 'mp'), may hold values from -6 to 6
- weight: bfloat16 [2, 12288, 12288], P('section', 'mp', 'dp'), may hold values from -1 to 1
- bias: float32 [2, 12288], P('section', 'dp'), may hold values from -3 to 3
- norm_gain: float32 [2, 12288], P('section', 'mp'), may hold values from 0.1 to 1.9
- norm_shift: float32 [2, 12288], P('section', 'mp'), may hold values from -3 to 3
Outputs:
- next_in: bfloat16 [2, 8, 8, 256, 1536], P('section', 'dp', 'mp')
- passed: bfloat16 [2, 8, 8, 256, 1536], P('section', 'dp', 'mp')
- weight_grad: float32 [2, 12288, 12288], P('section', 'mp', 'dp')
- bias_grad: float32 [2, 12288], P('section', 'dp')
- norm_grads: float32 [2, 2, 12288], P('section', None, 'mp')
All inputs are finite; a program needn't handle non-finite values.
Results may differ from a plain program's by a relative error of at most 0.018.
Values may be sent and summed in bfloat16 or wider, within the bound.
A program may use at most 128 MiB of HBM per device.

v0:
```python
import jax
import jax.numpy as jnp
from jax import lax
from jax.sharding import PartitionSpec as P

eps = 1e-05


def from_partner(value, axis, stride):
    mask = 2**stride
    pairs = [(source, source ^ mask) for source in range(lax.axis_size(axis))]
    return lax.ppermute(value, axis, pairs)


def standardize(values, totals, squares, full_width):
    mean_val = totals / full_width
    spread = squares / full_width - mean_val * mean_val
    inv_std = lax.rsqrt(spread + eps)
    return ((values - mean_val[:, None]) * inv_std[:, None], inv_std)


def regroup(outgoing, groups):
    flat_buffer = outgoing.reshape((groups * groups,) + outgoing.shape[2:])
    moved_data = lax.all_to_all(flat_buffer, ("dp", "mp"), split_axis=0, concat_axis=0, tiled=True)
    return moved_data.reshape(outgoing.shape)


def shards(fwd_in, kept_in, cotangent, weight, bias, norm_gain, norm_shift):
    section_index = lax.axis_index("section")
    groups = lax.axis_size("dp")
    row_count = fwd_in.shape[3]
    col_count = fwd_in.shape[4]
    full_width = col_count * lax.axis_size("mp")
    piece_rows = row_count // groups
    piece_cols = col_count // groups
    weight_tile = weight.reshape(col_count, col_count)
    gain_cols = norm_gain.reshape(col_count)
    shift_cols = norm_shift.reshape(col_count)
    fresh_rows = fwd_in.reshape(row_count, col_count).astype(jnp.float32)
    kept_values = kept_in.reshape(row_count, col_count).astype(jnp.float32)
    upstream = cotangent.reshape(row_count, col_count)
    row_stats = lax.psum(
        (
            jnp.sum(fresh_rows, 1),
            jnp.sum(fresh_rows * fresh_rows, 1),
            jnp.sum(kept_values, 1),
            jnp.sum(kept_values * kept_values, 1),
        ),
        "mp",
    )
    fresh_hat, unused_scale = standardize(fresh_rows, row_stats[0], row_stats[1], full_width)
    kept_hat, kept_inv = standardize(kept_values, row_stats[2], row_stats[3], full_width)
    normed = (fresh_hat * gain_cols + shift_cols).astype(jnp.bfloat16)
    normed_kept = (kept_hat * gain_cols + shift_cols).astype(jnp.bfloat16)
    upstream_all = lax.all_gather(upstream, "mp", axis=0, tiled=True)
    gathered, gathered_kept = (
        lax.all_gather(normed, "dp", axis=0, tiled=True),
        lax.all_gather(normed_kept, "dp", axis=0, tiled=True),
    )
    weight_grad = lax.dot_general(
        gathered_kept, upstream_all, (((0,), (0,)), ((), ())), preferred_element_type=jnp.float32
    )
    segment = gathered
    summed = lax.psum_scatter(
        jnp.dot(segment, weight_tile, preferred_element_type=jnp.float32).astype(jnp.bfloat16),
        "mp",
        scatter_dimension=0,
        tiled=True,
    ).astype(jnp.float32)
    output = (summed + bias.reshape(col_count)).astype(jnp.bfloat16)
    bias_grad = jnp.sum(upstream_all, 0, dtype=jnp.float32)
    segment = upstream_all
    grad_rows = lax.psum_scatter(
        lax.dot_general(
            segment, weight_tile, (((1,), (1,)), ((), ())), preferred_element_type=jnp.float32
        ).astype(jnp.bfloat16),
        "dp",
        scatter_dimension=0,
        tiled=True,
    ).astype(jnp.float32)
    scaled = grad_rows * gain_cols
    column_grads = lax.psum((jnp.sum(grad_rows * kept_hat, 0), jnp.sum(grad_rows, 0)), "dp")
    row_terms = lax.psum((jnp.sum(scaled, 1), jnp.sum(scaled * kept_hat, 1)), "mp")
    input_grad = (
        kept_inv[:, None]
        * (
            scaled
            - row_terms[0][:, None] / full_width
            - kept_hat * (row_terms[1][:, None] / full_width)
        )
    ).astype(jnp.bfloat16)
    out_pack = output.reshape(groups, piece_rows, groups, piece_cols).transpose(0, 2, 1, 3)
    grad_pack = input_grad.reshape(groups, piece_rows, groups, piece_cols).transpose(2, 0, 1, 3)
    outgoing = jnp.where(section_index == 0, out_pack, grad_pack)
    arrived = from_partner(regroup(outgoing, groups), "section", 0)
    as_cotangent = arrived.transpose(0, 2, 1, 3).reshape(row_count, col_count)
    as_input = arrived.transpose(1, 2, 0, 3).reshape(row_count, col_count)
    next_in = jnp.where(section_index == 0, as_cotangent, as_input)
    passed = jnp.where(section_index == 0, input_grad, output)
    return (
        next_in.reshape(fwd_in.shape),
        passed.reshape(fwd_in.shape),
        weight_grad.reshape(1, col_count, col_count),
        bias_grad.reshape(1, col_count),
        jnp.stack([column_grads[0], column_grads[1]]).reshape(1, 2, col_count),
    )


def solution(mesh):
    placed = (
        P("section", "dp", "mp", None, None),
        P("section", "dp", "mp", None, None),
        P("section", "dp", "mp", None, None),
        P("section", "mp", "dp"),
        P("section", "dp"),
        P("section", "mp"),
        P("section", "mp"),
    )
    return jax.shard_map(
        shards,
        mesh=mesh,
        in_specs=placed,
        out_specs=(
            P("section", "dp", "mp", None, None),
            P("section", "dp", "mp", None, None),
            P("section", "mp", "dp"),
            P("section", "dp"),
            P("section", None, "mp"),
        ),
        check_vma=False,
    )
```

profile of v0, /device:TPU:0, one launch (start us, length us, event | category | flops | bytes accessed | tf_op | source)
XLA Modules:
  0.0 515.9 jit_solution(15626368486175228471)
XLA Ops:
  7.2 0.0 all-gather.9.cloned.1.call-start
  7.2 0.7 all-gather.9.cloned.1.call-update
  7.9 0.0 reduce-scatter.5.cloned.1.call-start
  7.9 76.4 %all-gather.9.cloned.1.call-done = bf16[1,1,1,2048,1536]{4,3,2,1,0:T(8,128)(2,1)} async-done(((bf16[1,1,1,256,1536]{4,3,2,1,0:T(8,128)(2,1)}), bf16[1,1,1,2048,1536]{4,3,2,1,0:T(8,128)(2,1)}) %all-gather.9.cloned.1.call-update) | async-done | bytes 6291472 | tf_op jit(solution)/shard_map/all_gather | solution.py:55
  84.4 15.1 %convolution_convert_fusion = bf16[2048,1536]{1,0:T(8,128)(2,1)} fusion(bf16[1,1,1,2048,1536]{4,3,2,1,0:T(8,128)(2,1)} %all-gather.9.cloned.1.call-done, bf16[1,1536,1536]{2,1,0:T(8,128)(2,1)} %param.10), kind=kOutput, calls=%fused_computation.2 | convolution fusion | flops 9666822144 | bytes 17301504 | tf_op jit(solution)/shard_map/dot_general | solution.py:74
  99.5 0.0 copy-start.4
  99.5 0.0 copy-start.5
  99.5 0.0 copy-start
  99.5 0.0 reduce-scatter.5.cloned.1.call-update
  99.5 0.0 copy-start.1
  99.5 0.0 all-gather.5.cloned.1.call-start
  99.6 0.6 copy-done.4
  100.2 0.0 copy-done.5
  100.2 0.4 copy-done
  100.7 0.2 convert_reduce_fusion.2
  100.8 0.2 fusion.16
  101.1 16.9 %all-reduce.1 = (f32[256]{0:T(256)S(1)}, f32[256]{0:T(256)S(1)}) all-reduce(f32[256]{0:T(256)S(1)} %convert_reduce_fusion.2, f32[256]{0:T(256)S(1)} %fusion.16), channel_id=1, replica_groups=mesh['section'=2,'dp'=8,'mp'=8] {'mp'}, use_global_device_ids=true, to_apply=%region_8.0 | all-reduce | flops 512 | bytes 4096 | tf_op jit(solution)/shard_map/psum | solution.py:42
  118.0 0.0 copy-done.1
  118.0 0.2 convert_reduce_fusion.3
  118.2 0.2 fusion.15
  118.4 78.7 %reduce-scatter.5.cloned.1.call-done = bf16[256,1536]{1,0:T(8,128)(2,1)} async-done(((bf16[2048,1536]{1,0:T(8,128)(2,1)}), bf16[256,1536]{1,0:T(8,128)(2,1)}) %reduce-scatter.5.cloned.1.call-update) | async-done | bytes 786448 | tf_op jit(solution)/shard_map/reduce_scatter | solution.py:73
  197.1 2.8 fusion.26
  199.9 18.7 %all-reduce = (f32[256]{0:T(256)S(1)}, f32[256]{0:T(256)S(1)}, f32[256]{0:T(256)S(1)}, f32[256]{0:T(256)S(1)}) all-reduce(f32[256]{0:T(256)S(1)} %get-tuple-element.6, f32[256]{0:T(256)S(1)} %get-tuple-element.7, f32[256]{0:T(256)S(1)} %fusion.15, f32[256]{0:T(256)S(1)} %convert_reduce_fusion.3), channel_id=1, replica_groups=mesh['section'=2,'dp'=8,'mp'=8] {'mp'}, use_global_device_ids=true, to_apply=%region_13.0 | all-reduce | flops 1024 | bytes 8192 | tf_op jit(solution)/shard_map/psum | solution.py:83
  218.5 1.2 fusion.14
  219.8 0.0 all-gather.5.cloned.1.call-update
  219.8 0.0 reduce-scatter.3.cloned.1.call-start
  219.9 85.9 %all-gather.5.cloned.1.call-done = bf16[2048,1536]{1,0:T(8,128)(2,1)} async-done(((bf16[256,1536]{1,0:T(8,128)(2,1)}), bf16[2048,1536]{1,0:T(8,128)(2,1)}) %all-gather.5.cloned.1.call-update) | async-done | bytes 6291472 | tf_op jit(solution)/shard_map/all_gather | solution.py:57
  305.7 15.0 %convolution_convert_fusion.1 = bf16[2048,1536]{1,0:T(8,128)(2,1)} fusion(bf16[2048,1536]{1,0:T(8,128)(2,1)} %all-gather.5.cloned.1.call-done, bf16[1,1536,1536]{2,1,0:T(8,128)(2,1)} %param.10), kind=kOutput, calls=%fused_computation.3 | convolution fusion | flops 9666822144 | bytes 17301504 | tf_op jit(solution)/shard_map/dot_general | solution.py:65
  320.7 0.0 copy-start.6
  320.8 0.0 copy-start.3
  320.8 0.0 reduce-scatter.3.cloned.1.call-update
  320.8 0.0 all-gather.7.cloned.1.call-start
  320.8 0.5 all-gather.7.cloned.1.call-update
  321.4 0.1 copy-done.6
  321.5 70.1 %reduce-scatter.3.cloned.1.call-done = bf16[256,1536]{1,0:T(8,128)(2,1)} async-done(((bf16[2048,1536]{1,0:T(8,128)(2,1)}), bf16[256,1536]{1,0:T(8,128)(2,1)}) %reduce-scatter.3.cloned.1.call-update) | async-done | bytes 786448 | tf_op jit(solution)/shard_map/reduce_scatter | solution.py:64
  391.6 0.0 copy-done.3
  391.6 3.1 select_bitcast_fusion
  394.6 0.0 copy-start.2
  394.6 0.8 reshape.77
  395.5 0.3 copy-done.2
  395.8 0.8 reshape.79
  396.6 1.4 bitcast_select_fusion.1
  398.0 8.0 %all-to-all-start = ((bf16[64,32,192]{2,1,0:T(8,128)(2,1)}), bf16[64,32,192]{2,1,0:T(8,128)(2,1)S(1)}, u32[]{:S(2)}, u32[]{:S(2)}) async-start(bf16[64,32,192]{2,1,0:T(8,128)(2,1)} %bitcast.80), calls=%async_computation.2 | async-start | bytes 2097152 | tf_op jit(solution)/shard_map/all_to_all | solution.py:24
  406.1 3.7 convert_reduce_fusion
  409.8 0.6 reshape.84
  410.4 47.8 %all-reduce.2 = (f32[1,1536]{1,0:T(1,128)S(1)}, f32[1,1536]{1,0:T(1,128)S(1)}) all-reduce(f32[1,1536]{1,0:T(1,128)S(1)} %stack.10, f32[1,1536]{1,0:T(1,128)S(1)} %stack.9), channel_id=1, replica_groups=mesh['section'=2,'dp'=8,'mp'=8] {'dp'}, use_global_device_ids=true, to_apply=%region_18.0 | all-reduce | flops 3072 | bytes 24576 | tf_op jit(solution)/shard_map/psum | solution.py:82
  458.2 0.6 maximum_bitcast_fusion
  458.8 0.0 all-to-all-done
  458.8 0.0 collective-permute-start
  458.8 32.5 %all-gather.7.cloned.1.call-done = bf16[2048,1536]{1,0:T(8,128)(2,1)} async-done(((bf16[256,1536]{1,0:T(8,128)(2,1)}), bf16[2048,1536]{1,0:T(8,128)(2,1)}) %all-gather.7.cloned.1.call-update) | async-done | bytes 6291472 | tf_op jit(solution)/shard_map/all_gather | solution.py:58
  491.3 15.5 %convolution_bitcast_fusion = f32[1,1536,1536]{2,1,0:T(8,128)} fusion(bf16[2048,1536]{1,0:T(8,128)(2,1)} %all-gather.7.cloned.1.call-done, bf16[1,1,1,2048,1536]{4,3,2,1,0:T(8,128)(2,1)} %all-gather.9.cloned.1.call-done), kind=kOutput, calls=%fused_computation.1 | convolution fusion | flops 9663676416 | bytes 22020096 | tf_op jit(solution)/shard_map/dot_general | solution.py:60
  506.8 0.0 collective-permute-done
  506.8 0.1 bitcast_select_fusion
  506.9 0.6 copy.20
  507.6 1.8 select_n.36
  (8 shorter events, 0.1 us)
Async XLA Ops:
  7.2 77.2 %all-gather.9.cloned.1.call-start = ((), (), s32[]{:S(2)}) async-start(), calls=%async_computation.7 | async-start | bytes 7077888 | tf_op jit(solution)/shard_map/all_gather | solution.py:55
  7.9 189.2 %reduce-scatter.5.cloned.1.call-start = ((), (), s32[]{:S(2)}) async-start(), calls=%async_computation.5 | async-start | bytes 7077888 | tf_op jit(solution)/shard_map/reduce_scatter | solution.py:73
  99.5 0.7 copy-start.4
  99.5 0.7 copy-start.5
  99.5 1.2 copy-start
  99.5 18.4 %copy-start.1 = (bf16[1,1,1,256,1536]{4,3,2,1,0:T(8,128)(2,1)S(1)}, bf16[1,1,1,256,1536]{4,3,2,1,0:T(8,128)(2,1)}, u32[]{:S(2)}) copy-start(bf16[1,1,1,256,1536]{4,3,2,1,0:T(8,128)(2,1)} %param.7) | copy-start | bytes 2359300
  99.5 206.2 %all-gather.5.cloned.1.call-start = ((), (), s32[]{:S(2)}) async-start(), calls=%async_computation.3 | async-start | bytes 7077888 | tf_op jit(solution)/shard_map/all_gather | solution.py:57
  219.8 171.8 %reduce-scatter.3.cloned.1.call-start = ((), (), s32[]{:S(2)}) async-start(), calls=%async_computation.4 | async-start | bytes 7077888 | tf_op jit(solution)/shard_map/reduce_scatter | solution.py:64
  320.7 0.7 copy-start.6
  320.8 70.8 %copy-start.3 = (bf16[256,1536]{1,0:T(8,128)(2,1)S(1)}, bf16[256,1536]{1,0:T(8,128)(2,1)}, u32[]{:S(2)}) copy-start(bf16[256,1536]{1,0:T(8,128)(2,1)} %reduce-scatter.5.cloned.1.call-done) | copy-start | bytes 2359300
  320.8 170.5 %all-gather.7.cloned.1.call-start = ((), (), s32[]{:S(2)}) async-start(), calls=%async_computation.6 | async-start | bytes 7077888 | tf_op jit(solution)/shard_map/all_gather | solution.py:58
  394.6 1.1 copy-start.2
  398.0 60.8 %all-to-all-start = ((bf16[64,32,192]{2,1,0:T(8,128)(2,1)}), bf16[64,32,192]{2,1,0:T(8,128)(2,1)S(1)}, u32[]{:S(2)}, u32[]{:S(2)}) async-start(bf16[64,32,192]{2,1,0:T(8,128)(2,1)} %bitcast.80), calls=%async_computation.2 | async-start | bytes 2097152 | tf_op jit(solution)/shard_map/all_to_all | solution.py:24
  458.8 48.0 %collective-permute-start = (bf16[8,8,32,192]{3,2,1,0:T(8,128)(2,1)S(1)}, bf16[8,8,32,192]{3,2,1,0:T(8,128)(2,1)S(1)}, u32[]{:S(2)}, u32[]{:S(2)}) collective-permute-start(bf16[8,8,32,192]{3,2,1,0:T(8,128)(2,1)S(1)} %bitcast.81), channel_id=1, source_target_pairs={{0,64},{64,0},{1,65},{65,1},{2,66},{66,2},{3,67},{67,3},{4,68},{68... | collective-permute-start | bytes 2359304 | tf_op jit(solution)/shard_map/ppermute | solution.py:12
Sparse Core Ops, SparseCore 0:
  9.6 74.7 all-gather.8
  99.6 97.4 reduce-scatter.4
  219.9 85.7 all-gather.4
  320.9 70.6 reduce-scatter.2
  394.3 96.9 all-gather.6
where the time goes:
time: 517 us; the launch traced here: 516 us
  waiting for transfers between devices  345 us (67%)
  blocking collectives  83.4 us (16%)
  matrix products  45.7 us (9%)
  between operations  13.9 us (3%)
  other arithmetic  13.8 us (3%)
  starting transfers between devices  8.22 us (2%)
  local copies, waits for them, and re-layouts  6.07 us (1%)
    all_gather x1, waiting for transfers between devices, shards(): lax.all_gather(normed, 'dp', axis=0, tiled=True)  85.9 us
    reduce_scatter x1, waiting for transfers between devices, shards(): lax.psum_scatter(lax.dot_general(segment, weight_tile, (((1,), (1,)), (()...  78.7 us
    all_gather x1, waiting for transfers between devices, shards(): upstream_all = lax.all_gather(upstream, 'mp', axis=0, tiled=True)  76.4 us
    reduce_scatter x1, waiting for transfers between devices, shards(): lax.psum_scatter(jnp.dot(segment, weight_tile, preferred_element_type=jnp...  70.1 us
    psum x1, blocking collectives, shards(): lax.psum((jnp.sum(grad_rows * kept_hat, 0), jnp.sum(grad_rows, 0)), 'dp')  47.8 us
    all_gather x1, waiting for transfers between devices, shards(): lax.all_gather(normed_kept, 'dp', axis=0, tiled=True)  32.5 us
    psum x1, blocking collectives, shards(): lax.psum((jnp.sum(scaled, 1), jnp.sum(scaled * kept_hat, 1)), 'mp')  18.7 us
    psum x1, blocking collectives, shards(): lax.psum((jnp.sum(fresh_rows, 1), jnp.sum(fresh_rows * fresh_rows, 1), jn...  16.9 us
  transfers between devices with their start and end apart: 7, of which 5 were waited for; matrix products, arithmetic and copies ran while one was open for 5% of the time, Pallas kernels for 0%

commit v1 on v0

v1 whole, which is shorter than its diff:
```python
import jax
import jax.numpy as jnp
from jax import lax
from jax.experimental import pallas as pl
from jax.experimental.pallas import tpu as pltpu
from jax.sharding import PartitionSpec as P

EPS = 1e-05
RING = 4
PAIR = 2
GROUP = RING * PAIR
TILE = 16
MXU = 256
F32 = jnp.float32
BF16 = jnp.bfloat16
MESH = pl.DeviceIdType.MESH


class Spot:
    def __init__(self, group):
        self.group = group
        self.index = lax.axis_index(group)
        self.pair = lax.div(self.index, RING)
        self.ring = lax.rem(self.index, RING)

    def slot(self, pair_step, ring_step):
        pair = lax.rem(self.pair + pair_step, PAIR)
        return pair * RING + lax.rem(self.ring + ring_step + RING, RING)

    def device(self, pair_step, ring_step):
        return {self.group: self.slot(pair_step, ring_step)}


class Gather:
    def __init__(self, spot, buf, send_sem, recv_sem, far_by_pair):
        self.spot, self.buf, self.far_by_pair = spot, buf, far_by_pair
        self.send_sem, self.recv_sem = send_sem, recv_sem
        self.half = buf.shape[1] // 2
        self.started = []

    def route(self, kind, c):
        step = 1 if c == 0 else -1
        return {
            0: ((0, 0), (1, 0), (1, 0)),
            1: ((0, 0), (0, 1), (0, -1)),
            2: ((0, 0), (0, -1), (0, 1)),
            3: ((1, 0), (0, 1), (1, -1)),
            4: ((1, 0), (0, -1), (1, 1)),
            5: ((0, -step), (0, step), (0, 2)),
            6: ((0, 2), (1, 0), (1, 2)) if self.far_by_pair else ((1, -step), (0, step), (1, 2)),
        }[kind]

    def copy(self, kind, c, landing):
        source, target, lands = self.route(kind, c)
        here = self.spot.slot(*(lands if landing else source))
        view = self.buf.at[here, pl.ds(c * self.half, self.half)]
        return pltpu.make_async_remote_copy(
            src_ref=view,
            dst_ref=view,
            send_sem=self.send_sem.at[kind, c],
            recv_sem=self.recv_sem.at[kind, c],
            device_id=self.spot.device(*target),
            device_id_type=MESH,
        )

    def start(self, kind, c):
        self.copy(kind, c, False).start()
        self.started.append((kind, c))

    def arrived(self, kind, c):
        self.copy(kind, c, True).wait_recv()

    def finish(self):
        for kind, c in self.started:
            self.copy(kind, c, False).wait_send()
        self.started = []


class Scatter:
    def __init__(self, spot, stage, halves, left, right, crossed, send_sem, recv_sem):
        self.spot, self.stage = spot, stage
        self.halves, self.left, self.right, self.crossed = halves, left, right, crossed
        self.send_sem, self.recv_sem = send_sem, recv_sem
        self.half = halves.shape[1] // 2
        self.started = []

    def copy(self, kind, side, c):
        spot, rows = self.spot, pl.ds(c * self.half, self.half)
        step = 1 if c == 0 else -1
        source, target, lands = {
            0: (self.stage(side, 2), (0, step), self.halves.at[side]),
            1: (self.stage(side, 1), (0, 1), self.left.at[side]),
            2: (self.stage(side, -1), (0, -1), self.right.at[side]),
            3: (self.stage(side, 0), (1, 0), self.crossed),
        }[kind]
        sem = (kind * 2 + side) * 2 + c
        return pltpu.make_async_remote_copy(
            src_ref=source.at[rows],
            dst_ref=lands.at[rows],
            send_sem=self.send_sem.at[sem],
            recv_sem=self.recv_sem.at[sem],
            device_id=spot.device(*target),
            device_id_type=MESH,
        )

    def start(self, kind, side, c):
        self.copy(kind, side, c).start()
        self.started.append((kind, side, c))

    def arrived(self, kind, side, c):
        self.copy(kind, side, c).wait_recv()

    def finish(self):
        for key in self.started:
            self.copy(*key).wait_send()
        self.started = []


class Spread:
    def __init__(self, spot, buf, send_sem, recv_sem):
        self.spot, self.buf, self.send_sem, self.recv_sem = spot, buf, send_sem, recv_sem

    def copy(self, step, landing):
        me = self.spot.index
        other = lax.rem(me + step, GROUP)
        view = self.buf.at[lax.rem(me + GROUP - step, GROUP) if landing else me]
        return pltpu.make_async_remote_copy(
            src_ref=view,
            dst_ref=view,
            send_sem=self.send_sem.at[step - 1],
            recv_sem=self.recv_sem.at[step - 1],
            device_id={self.spot.group: other},
            device_id_type=MESH,
        )

    def start(self):
        for step in range(1, GROUP):
            self.copy(step, False).start()

    def arrived(self):
        for step in range(1, GROUP):
            self.copy(step, True).wait_recv()

    def finish(self):
        for step in range(1, GROUP):
            self.copy(step, False).wait_send()

    def total(self):
        result = self.buf[0]
        for i in range(1, GROUP):
            result = result + self.buf[i]
        return result


def tiles(count, body, size=TILE):
    def step(i, carry):
        body(pl.ds(pl.multiple_of(i * size, size), size))
        return carry

    lax.fori_loop(0, count // size, step, 0)


def relay_kernel(
    fwd, kept, cot, weight, bias, gain, shift,
    arrived_out, passed_out, wg_out, bg_out, ng_out,
    xs, ks, cs, w, kown, wg, gst, hhalf, hleft, hright, hcross, ghalf, gleft, gright, gcross,
    vblk, acc, yout, cols, stat, fin, rowt, colg, bsum, pack, land,
    loc_sem, wg_sem,
    c_ss, c_rs, x_ss, x_rs, k_ss, k_rs, h_ss, h_rs, g_ss, g_rs,
    stat_ss, stat_rs, fin_ss, fin_rs, rowt_ss, rowt_rs, colg_ss, colg_rs, a_ss, a_rs,
):
    section = lax.axis_index("section")
    dp, mp = Spot("dp"), Spot("mp")
    rows, width = fwd.shape
    full = width * GROUP
    n_blocks = width // MXU

    loads = [
        pltpu.make_async_copy(cot, cs.at[mp.index], loc_sem.at[0]),
        pltpu.make_async_copy(fwd, xs.at[dp.index], loc_sem.at[1]),
        pltpu.make_async_copy(kept, ks.at[dp.index], loc_sem.at[2]),
        pltpu.make_async_copy(kept, kown, loc_sem.at[3]),
        pltpu.make_async_copy(weight, w, loc_sem.at[4]),
    ]
    for load in loads:
        load.start()

    barrier = pltpu.get_barrier_semaphore()
    for spot in (mp, dp):
        for step in range(1, GROUP):
            pl.semaphore_signal(
                barrier, inc=1, device_id={spot.group: lax.rem(spot.index + step, GROUP)}, device_id_type=MESH
            )

    def greet(i, carry):
        pl.semaphore_signal(
            barrier,
            inc=1,
            device_id={"section": 1 - section, "dp": lax.div(i, GROUP), "mp": lax.rem(i, GROUP)},
            device_id_type=MESH,
        )
        return carry

    lax.fori_loop(0, GROUP * GROUP, greet, 0)
    pl.semaphore_wait(barrier, 2 * (GROUP - 1) + GROUP * GROUP)

    gc = Gather(mp, cs, c_ss, c_rs, False)
    gx = Gather(dp, xs, x_ss, x_rs, True)
    gk = Gather(dp, ks, k_ss, k_rs, True)
    loads[0].wait()
    for c in (0, 1):
        for kind in (0, 1, 2):
            gc.start(kind, c)
    loads[1].wait()
    for c in (0, 1):
        for kind in (0, 1, 2):
            gx.start(kind, c)

    loads[2].wait()
    lane = lax.broadcasted_iota(jnp.int32, (TILE, 128), 1)

    def in_lanes(values):
        result = jnp.zeros((TILE, 128), F32)
        for i, value in enumerate(values):
            result = jnp.where(lane == i, value, result)
        return result

    def row_sums(at):
        x = xs[dp.index, at].astype(F32)
        k = ks[dp.index, at].astype(F32)
        sums = [jnp.sum(v, 1, keepdims=True) for v in (x, x * x, k, k * k)]
        cols[at] = in_lanes(sums)

    tiles(rows, row_sums)
    stats = Spread(mp, stat, stat_ss, stat_rs)
    stat[mp.index] = jnp.transpose(cols[...])[0:8]
    stats.start()
    stats.arrived()
    sums = stats.total() / full
    mean_x, mean_k = sums[0:1], sums[2:3]
    inv_x = lax.rsqrt(sums[1:2] - mean_x * mean_x + EPS)
    inv_k = lax.rsqrt(sums[3:4] - mean_k * mean_k + EPS)
    row = lax.broadcasted_iota(jnp.int32, (8, rows), 0)
    fin[dp.index] = jnp.where(row == 0, mean_x, jnp.where(row == 1, inv_x, jnp.where(row == 2, mean_k, inv_k)))
    finished = Spread(dp, fin, fin_ss, fin_rs)
    finished.start()

    def forward(gather):
        gather.arrived(1, 0)
        gather.start(5, 0)
        gather.arrived(2, 1)
        gather.start(5, 1)

    forward(gc)
    forward(gx)
    for c in (0, 1):
        for gather in (gc, gx):
            gather.arrived(0, c)
            gather.start(3, c)
            gather.start(4, c)
    for c in (0, 1):
        gx.arrived(5, c)
        gx.start(6, c)
    gc.arrived(3, 0)
    gc.start(6, 0)
    gc.arrived(4, 1)
    gc.start(6, 1)
    for c in (0, 1):
        gk.start(1, c)
        gk.start(2, c)
    for kind, c in ((1, 1), (2, 0), (3, 0), (3, 1), (4, 0), (4, 1), (6, 0), (6, 1)):
        gx.arrived(kind, c)
    finished.arrived()
    loads[4].wait()
    gx.finish()
    for kind, c in ((1, 1), (2, 0), (3, 1), (4, 0), (5, 0), (5, 1), (6, 0), (6, 1)):
        gc.arrived(kind, c)
    loads[3].wait()

    def normalise(buf, slot, out, which):
        cols[:, 0:8] = jnp.transpose(fin[slot])

        def body(at):
            mean = cols[at, which : which + 1]
            inv = cols[at, which + 1 : which + 2]
            hat = (buf[slot, at].astype(F32) - mean) * inv
            out[at] = (hat * gain[...] + shift[...]).astype(BF16)

        tiles(rows, body)

    bsum[...] = jnp.zeros_like(bsum)

    def product_h(slot):
        normalise(xs, slot, xs.at[slot], 0)

        def body(n, carry):
            at = pl.ds(pl.multiple_of(n * MXU, MXU), MXU)
            acc[:, at] = jnp.dot(xs[slot], w[:, at], preferred_element_type=F32)
            return carry

        lax.fori_loop(0, n_blocks, body, 0)

    def product_g(slot):
        def body(n, carry):
            at = pl.ds(pl.multiple_of(n * MXU, MXU), MXU)
            acc[:, at] = lax.dot_general(
                cs[slot], w[at, :], (((1,), (1,)), ((), ())), preferred_element_type=F32
            )
            return carry

        lax.fori_loop(0, n_blocks, body, 0)

        def add(at):
            c = cs[slot, at].astype(F32)
            bsum[...] += c[0:8] + c[8:16]

        tiles(rows, add)

    half = rows // 2

    def emit(stage, start, terms):
        def body(i, carry):
            at = pl.ds(pl.multiple_of(start + i * TILE, TILE), TILE)
            value = acc[at]
            for term in terms:
                value = value + term[at].astype(F32)
            stage[at] = value.astype(BF16)
            return carry

        lax.fori_loop(0, half // TILE, body, 0)

    def stage_g(side, ring_step):
        place = {2: 0, 1: 1, -1: 2, 0: 3}[ring_step] * 2 + side
        return gst.at[place]

    def stage_h(side, ring_step):
        return xs.at[mp.slot(1 - side, ring_step)]

    rg = Scatter(dp, stage_g, ghalf, gleft, gright, gcross, g_ss, g_rs)
    rh = Scatter(mp, stage_h, hhalf, hleft, hright, hcross, h_ss, h_rs)
    work = ((rg, product_g), (rh, product_h))

    for side in (0, 1):
        for scatter, product in work:
            product(scatter.spot.slot(1 - side, 2))
            for c in (0, 1):
                emit(scatter.stage(side, 2), c * half, [])
                scatter.start(0, side, c)
    for c in (0, 1):
        gk.start(0, c)
    for side in (0, 1):
        for scatter, product in work:
            product(scatter.spot.slot(1 - side, 1))
            emit(scatter.stage(side, 1), half, [])
            scatter.start(1, side, 1)
            scatter.arrived(0, side, 0)
            emit(scatter.stage(side, 1), 0, [scatter.halves.at[side]])
            scatter.start(1, side, 0)
            product(scatter.spot.slot(1 - side, -1))
            emit(scatter.stage(side, -1), 0, [])
            scatter.start(2, side, 0)
            scatter.arrived(0, side, 1)
            emit(scatter.stage(side, -1), half, [scatter.halves.at[side]])
            scatter.start(2, side, 1)
    forward(gk)
    for c in (0, 1):
        gk.arrived(0, c)
        gk.start(3, c)
        gk.start(4, c)
    for scatter, product in work:
        product(scatter.spot.slot(1, 0))
        for c in (0, 1):
            scatter.arrived(1, 0, c)
            scatter.arrived(2, 0, c)
            emit(scatter.stage(0, 0), c * half, [scatter.left.at[0], scatter.right.at[0]])
            scatter.start(3, 0, c)
    for c in (0, 1):
        gk.arrived(5, c)
        gk.start(6, c)

    def whole(scatter, finish):
        for c in (0, 1):
            for kind, side in ((1, 1), (2, 1), (3, 0)):
                scatter.arrived(kind, side, c)

        def body(at):
            value = acc[at]
            for term in (scatter.left.at[1], scatter.right.at[1], scatter.crossed):
                value = value + term[at].astype(F32)
            finish(at, value)

        tiles(rows, body)

    def finish_h(at, value):
        yout[at] = (value + bias[...]).astype(BF16)

    product_h(mp.slot(0, 0))
    whole(rh, finish_h)

    product_g(dp.slot(0, 0))
    cols[:, 0:8] = jnp.transpose(fin[dp.index])
    colg[dp.index] = jnp.zeros(colg.shape[1:], F32)

    def hat_kept(at):
        return (kown[at].astype(F32) - cols[at, 2:3]) * cols[at, 3:4]

    def finish_g(at, value):
        hat = hat_kept(at)
        colg[dp.index, 0:1] += jnp.sum(value * hat, 0, keepdims=True)
        colg[dp.index, 1:2] += jnp.sum(value, 0, keepdims=True)
        acc[at] = value
        scaled = value * gain[...]
        terms = [jnp.sum(v, 1, keepdims=True) for v in (scaled, scaled * hat)]
        lanes = in_lanes([terms[0], terms[1]])
        cols[at, 8:16] = lanes[:, 0:8]

    whole(rg, finish_g)
    column = Spread(dp, colg, colg_ss, colg_rs)
    column.start()
    terms = Spread(mp, rowt, rowt_ss, rowt_rs)
    rowt[mp.index] = jnp.transpose(cols[...])[8:16]
    terms.start()
    terms.arrived()
    cols[:, 8:16] = jnp.transpose(terms.total() / full)

    def input_grad(at):
        hat = hat_kept(at)
        scaled = acc[at] * gain[...]
        grad = cols[at, 3:4] * (scaled - cols[at, 8:9] - hat * cols[at, 9:10])
        acc[at] = grad

    tiles(rows, input_grad)

    piece_rows, piece_cols = pack.shape[2:]

    def packing(b, carry):
        at = pl.ds(pl.multiple_of(b * piece_rows, piece_rows), piece_rows)
        out = yout[at].astype(F32)
        grad = acc[at]
        sent = jnp.where(section == 0, out, grad)
        yout[at] = jnp.where(section == 0, grad, out).astype(BF16)
        for f in range(GROUP):
            pack[b, f] = sent[:, f * piece_cols : (f + 1) * piece_cols].astype(BF16)
        return carry

    lax.fori_loop(0, GROUP, packing, 0)
    first = section == 0
    row_at = jnp.where(first, mp.index, dp.index)
    col_at = jnp.where(first, dp.index, mp.index)

    def piece(i):
        j = lax.rem(i + dp.index * GROUP + mp.index, GROUP * GROUP)
        b, f = lax.div(j, GROUP), lax.rem(j, GROUP)
        return pltpu.make_async_remote_copy(
            src_ref=pack.at[b, f],
            dst_ref=land.at[row_at, col_at],
            send_sem=a_ss.at[j],
            recv_sem=a_rs.at[row_at * GROUP + col_at],
            device_id={"section": 1 - section, "dp": jnp.where(first, b, f), "mp": jnp.where(first, f, b)},
            device_id_type=MESH,
        )

    def send_piece(i, carry):
        piece(i).start()
        return carry

    lax.fori_loop(0, GROUP * GROUP, send_piece, 0)
    keep = pltpu.make_async_copy(yout, passed_out, loc_sem.at[0])
    keep.start()

    wg[...] = jnp.zeros_like(wg)

    def product_w(slot):
        normalise(ks, slot, vblk, 2)

        def body(n, carry):
            at = pl.ds(pl.multiple_of(n * MXU, MXU), MXU)
            wg[at, :] += lax.dot_general(
                vblk[:, at], cs[slot], (((0,), (0,)), ((), ())), preferred_element_type=F32
            )
            return carry

        lax.fori_loop(0, n_blocks, body, 0)

    for kind, c in ((1, 1), (2, 0)):
        gk.arrived(kind, c)
    for pair_step, ring_step, kinds in (
        (0, 0, ()), (1, 0, ()), (0, 1, ()), (0, -1, ()), (0, 2, ()), (1, 1, (4,)), (1, -1, (3,)), (1, 2, (6,))
    ):
        for kind in kinds:
            for c in (0, 1):
                gk.arrived(kind, c)
        product_w(dp.slot(pair_step, ring_step))
    store = pltpu.make_async_copy(wg, wg_out, wg_sem)
    store.start()

    bg_out[...] = jnp.sum(bsum[...], 0, keepdims=True)
    column.arrived()
    ng_out[...] = column.total()

    def landed(i, carry):
        pltpu.make_async_remote_copy(
            src_ref=pack.at[0, 0],
            dst_ref=land.at[lax.div(i, GROUP), lax.rem(i, GROUP)],
            send_sem=a_ss.at[i],
            recv_sem=a_rs.at[i],
            device_id={"section": 1 - section},
            device_id_type=MESH,
        ).wait_recv()
        return carry

    lax.fori_loop(0, GROUP * GROUP, landed, 0)
    out = pltpu.make_async_copy(land, arrived_out, loc_sem.at[1])
    out.start()

    def left(i, carry):
        piece(i).wait_send()
        return carry

    lax.fori_loop(0, GROUP * GROUP, left, 0)
    for transfer in (gc, gk, rg, rh, stats, finished, column, terms):
        transfer.finish()
    keep.wait()
    store.wait()
    out.wait()


def shards(fwd_in, kept_in, cotangent, weight, bias, norm_gain, norm_shift):
    section_index = lax.axis_index("section")
    rows, cols = fwd_in.shape[3:]
    piece = (GROUP, GROUP, rows // GROUP, cols // GROUP)
    any_spec = pl.BlockSpec(memory_space=pl.ANY)
    vmem_spec = pl.BlockSpec(memory_space=pltpu.VMEM)
    dma = pltpu.SemaphoreType.DMA
    shard = pltpu.VMEM((rows, cols), BF16)
    gathered = pltpu.VMEM((GROUP, rows, cols), BF16)
    two = pltpu.VMEM((2, rows, cols), BF16)
    arrived, passed, weight_grad, bias_grad, norm_grads = pl.pallas_call(
        relay_kernel,
        name="relay",
        out_shape=(
            jax.ShapeDtypeStruct(piece, BF16),
            jax.ShapeDtypeStruct((rows, cols), BF16),
            jax.ShapeDtypeStruct((cols, cols), F32),
            jax.ShapeDtypeStruct((1, cols), F32),
            jax.ShapeDtypeStruct((2, cols), F32),
        ),
        in_specs=[any_spec] * 4 + [vmem_spec] * 3,
        out_specs=(any_spec, any_spec, any_spec, vmem_spec, vmem_spec),
        scratch_shapes=[
            gathered, gathered, gathered, pltpu.VMEM((cols, cols), BF16), shard, pltpu.VMEM((cols, cols), F32),
            pltpu.VMEM((7, rows, cols), BF16),
            two, two, two, shard, two, two, two, shard,
            shard, pltpu.VMEM((rows, cols), F32), shard, pltpu.VMEM((rows, 128), F32),
            pltpu.VMEM((GROUP, 8, rows), F32), pltpu.VMEM((GROUP, 8, rows), F32), pltpu.VMEM((GROUP, 8, rows), F32),
            pltpu.VMEM((GROUP, 2, cols), F32), pltpu.VMEM((8, cols), F32),
            pltpu.VMEM(piece, BF16), pltpu.VMEM(piece, BF16),
            dma((5,)), dma,
            dma((7, 2)), dma((7, 2)), dma((7, 2)), dma((7, 2)), dma((7, 2)), dma((7, 2)),
            dma((16,)), dma((16,)), dma((16,)), dma((16,)),
            dma((7,)), dma((7,)), dma((7,)), dma((7,)), dma((7,)), dma((7,)), dma((7,)), dma((7,)),
            dma((GROUP * GROUP,)), dma((GROUP * GROUP,)),
        ],
        compiler_params=pltpu.CompilerParams(
            collective_id=0, has_side_effects=True, vmem_limit_bytes=60 * 2**20
        ),
    )(
        fwd_in.reshape(rows, cols),
        kept_in.reshape(rows, cols),
        cotangent.reshape(rows, cols),
        weight.reshape(cols, cols),
        bias.reshape(1, cols),
        norm_gain.reshape(1, cols),
        norm_shift.reshape(1, cols),
    )
    next_in = arrived.transpose(0, 2, 1, 3).reshape(fwd_in.shape)
    return (
        next_in,
        passed.reshape(fwd_in.shape),
        weight_grad.reshape(1, cols, cols),
        bias_grad,
        norm_grads.reshape(1, 2, cols),
    )


def solution(mesh):
    placed = (
        P("section", "dp", "mp", None, None),
        P("section", "dp", "mp", None, None),
        P("section", "dp", "mp", None, None),
        P("section", "mp", "dp"),
        P("section", "dp"),
        P("section", "mp"),
        P("section", "mp"),
    )
    return jax.shard_map(
        shards,
        mesh=mesh,
        in_specs=placed,
        out_specs=(
            P("section", "dp", "mp", None, None),
            P("section", "dp", "mp", None, None),
            P("section", "mp", "dp"),
            P("section", "dp"),
            P("section", None, "mp"),
        ),
        check_vma=False,
    )
```

time: 517 us -> 243 us (0.47)
  waiting for transfers between devices: 345 us -> 0 us
  Pallas kernels: 0 us -> 227 us
  blocking collectives: 83.4 us -> 0 us
  matrix products: 45.7 us -> 0 us
  other arithmetic: 13.8 us -> 0 us
  between operations: 13.9 us -> 0.65 us
  local copies, waits for them, and re-layouts: 6.07 us -> 15.2 us
  starting transfers between devices: 8.22 us -> 0 us
    pallas_call x0 -> x1, Pallas kernels: none -> 227 us  [shards(): pl.pallas_call(relay_kernel, name='relay', out_shape=(jax.ShapeDtypeStruc...]
    all_gather x3 -> x0, waiting for transfers between devices: 195 us -> none  [the longest x1 85.9 us: shards(): lax.all_gather(normed, 'dp', axis=0, tiled=True)]
    reduce_scatter x2 -> x0, waiting for transfers between devices: 149 us -> none  [the longest x1 78.7 us: shards(): lax.psum_scatter(lax.dot_general(segment, weight_tile, (((1,), (1,)), (()...]
    psum x3 -> x0, blocking collectives: 83.4 us -> none  [the longest x1 47.8 us: shards(): lax.psum((jnp.sum(grad_rows * kept_hat, 0), jnp.sum(grad_rows, 0)), 'dp')]
    dot_general x3 -> x0, matrix products: 45.7 us -> none  [the longest x1 15.5 us: shards(): lax.dot_general(gathered_kept, upstream_all, (((0,), (0,)), ((), ())), pr...]
    unnamed x14 -> x8, local copies, waits for them, and re-layouts: 1.4 us -> 11.6 us
    all_to_all x1 -> x0, starting transfers between devices: 8.02 us -> none  [regroup(): lax.all_to_all(flat_buffer, ('dp', 'mp'), split_axis=0, concat_axis=0, ti...]
    reduce_sum x6 -> x0, other arithmetic: 7.3 us -> none  [the longest x1 3.72 us: shards(): bias_grad = jnp.sum(upstream_all, 0, dtype=jnp.float32)]
  transfers between devices with their start and end apart: 7 -> 0, of which waited for: 5 -> 0; matrix products, arithmetic and copies ran while one was open for 5% -> 0% of each run, Pallas kernels for 0% -> 0%
where the time goes in v1:
time: 243 us
  Pallas kernels  227 us (93%)
  local copies, waits for them, and re-layouts  15.2 us (6%)
    pallas_call x1, Pallas kernels, shards(): pl.pallas_call(relay_kernel, name='relay', out_shape=(jax.ShapeDtypeStruc...  227 us
    unnamed x8, local copies, waits for them, and re-layouts  11.6 us

profile of v1, /device:TPU:0, one launch (start us, length us, event | category | flops | bytes accessed | tf_op | source)
XLA Modules:
  0.0 242.8 jit_solution(1714428181594968060)
XLA Ops:
  0.6 226.9 %relay.1 = (bf16[8,8,32,192]{3,2,1,0:T(8,128)(2,1)}, bf16[256,1536]{1,0:T(8,128)(2,1)}, f32[1536,1536]{1,0:T(8,128)}, f32[1,1536]{1,0:T(1,128)}, f32[2,1536]{1,0:T(2,128)}) custom-call(bf16[256,1536]{1,0:T(8,128)(2,1)} %bitcast.14, bf16[256,1536]{1,0:T(8,128)(2,1)} %bitcast.15, bf16[256,1536]{1,0:T(8,128)(2,1)} %bitcast.16, bf16[1536,1536]{1,0:T(8,128)(2,1)} %bitcast.11, ...), custom_call_target="tpu_custom_call" | custom-call | tf_op jit(solution)/shard_map/relay/pallas_call | solution.py:538
  227.6 1.9 copy.12
  229.4 1.8 reshape.38
  231.2 2.1 copy.17
  233.3 0.0 copy-start.1
  233.3 0.0 copy-start
  233.3 8.3 %copy.18 = f32[1,1536,1536]{2,1,0:T(8,128)} copy(f32[1,1536,1536]{2,1,0:T(8,128)} %bitcast.10) | data formatting | bytes 18874368
  241.6 0.0 copy-done.1
  241.6 0.6 copy.19
  242.2 0.0 copy-done
  242.2 0.6 copy.20
Async XLA Ops:
  233.3 8.3 %copy-start.1 = (f32[1,1536]{1,0:T(1,128)S(1)}, f32[1,1536]{1,0:T(1,128)}, u32[]{:S(2)}) copy-start(f32[1,1536]{1,0:T(1,128)} %get-tuple-element.23) | copy-start | bytes 18436
  233.3 8.9 %copy-start = (f32[2,1536]{1,0:T(2,128)S(1)}, f32[2,1536]{1,0:T(2,128)}, u32[]{:S(2)}) copy-start(f32[2,1536]{1,0:T(2,128)} %get-tuple-element.14) | copy-start | bytes 36868

commit v2 on v1

--- a/solution.py
+++ b/solution.py
@@ -10,6 +10,7 @@
 PAIR = 2
 GROUP = RING * PAIR
 TILE = 16
+LATE = ((4, 1, 1), (3, 1, -1), (6, 1, 2))
 MXU = 256
 F32 = jnp.float32
 BF16 = jnp.bfloat16
@@ -69,6 +70,11 @@
 
     def arrived(self, kind, c):
         self.copy(kind, c, True).wait_recv()
+
+    def sent(self, kind):
+        for c in (0, 1):
+            self.copy(kind, c, False).wait_send()
+            self.started.remove((kind, c))
 
     def finish(self):
         for kind, c in self.started:
@@ -157,15 +163,15 @@
         body(pl.ds(pl.multiple_of(i * size, size), size))
         return carry
 
-    lax.fori_loop(0, count // size, step, 0)
+    lax.fori_loop(0, count // size, step, 0, unroll=4)
 
 
 def relay_kernel(
     fwd, kept, cot, weight, bias, gain, shift,
-    arrived_out, passed_out, wg_out, bg_out, ng_out,
+    arrived_out, passed_out, wg_out, v_out, c_out, bg_out, ng_out,
     xs, ks, cs, w, kown, wg, gst, hhalf, hleft, hright, hcross, ghalf, gleft, gright, gcross,
-    vblk, acc, yout, cols, stat, fin, rowt, colg, bsum, pack, land,
-    loc_sem, wg_sem,
+    vblk, acc, accg, yout, cols, stat, fin, rowt, colg, bsum, pack, land,
+    loc_sem, wg_sem, late_sem,
     c_ss, c_rs, x_ss, x_rs, k_ss, k_rs, h_ss, h_rs, g_ss, g_rs,
     stat_ss, stat_rs, fin_ss, fin_rs, rowt_ss, rowt_rs, colg_ss, colg_rs, a_ss, a_rs,
 ):
@@ -173,7 +179,7 @@
     dp, mp = Spot("dp"), Spot("mp")
     rows, width = fwd.shape
     full = width * GROUP
-    n_blocks = width // MXU
+    wide = width // 2
 
     loads = [
         pltpu.make_async_copy(cot, cs.at[mp.index], loc_sem.at[0]),
@@ -182,8 +188,8 @@
         pltpu.make_async_copy(kept, kown, loc_sem.at[3]),
         pltpu.make_async_copy(weight, w, loc_sem.at[4]),
     ]
-    for load in loads:
-        load.start()
+    for i in (1, 2, 0):
+        loads[i].start()
 
     barrier = pltpu.get_barrier_semaphore()
     for spot in (mp, dp):
@@ -192,31 +198,8 @@
                 barrier, inc=1, device_id={spot.group: lax.rem(spot.index + step, GROUP)}, device_id_type=MESH
             )
 
-    def greet(i, carry):
-        pl.semaphore_signal(
-            barrier,
-            inc=1,
-            device_id={"section": 1 - section, "dp": lax.div(i, GROUP), "mp": lax.rem(i, GROUP)},
-            device_id_type=MESH,
-        )
-        return carry
-
-    lax.fori_loop(0, GROUP * GROUP, greet, 0)
-    pl.semaphore_wait(barrier, 2 * (GROUP - 1) + GROUP * GROUP)
-
-    gc = Gather(mp, cs, c_ss, c_rs, False)
-    gx = Gather(dp, xs, x_ss, x_rs, True)
-    gk = Gather(dp, ks, k_ss, k_rs, True)
-    loads[0].wait()
-    for c in (0, 1):
-        for kind in (0, 1, 2):
-            gc.start(kind, c)
-    loads[1].wait()
-    for c in (0, 1):
-        for kind in (0, 1, 2):
-            gx.start(kind, c)
-
-    loads[2].wait()
+    pl.semaphore_signal(barrier, inc=1, device_id={"section": 1 - section}, device_id_type=MESH)
+
     lane = lax.broadcasted_iota(jnp.int32, (TILE, 128), 1)
 
     def in_lanes(values):
@@ -231,10 +214,25 @@
         sums = [jnp.sum(v, 1, keepdims=True) for v in (x, x * x, k, k * k)]
         cols[at] = in_lanes(sums)
 
+    loads[1].wait()
+    loads[2].wait()
     tiles(rows, row_sums)
+    stat[mp.index] = jnp.transpose(cols[...])[0:8]
+    loads[0].wait()
+    pl.semaphore_wait(barrier, 2 * (GROUP - 1) + 1)
+
+    gc = Gather(mp, cs, c_ss, c_rs, False)
+    gx = Gather(dp, xs, x_ss, x_rs, True)
+    gk = Gather(dp, ks, k_ss, k_rs, True)
     stats = Spread(mp, stat, stat_ss, stat_rs)
-    stat[mp.index] = jnp.transpose(cols[...])[0:8]
     stats.start()
+    for c in (0, 1):
+        for gather in (gc, gx):
+            gather.start(0, c)
+            gather.start(1, c)
+            gather.start(2, 1 - c)
+    loads[4].start()
+    loads[3].start()
     stats.arrived()
     sums = stats.total() / full
     mean_x, mean_k = sums[0:1], sums[2:3]
@@ -251,31 +249,23 @@
         gather.arrived(2, 1)
         gather.start(5, 1)
 
-    forward(gc)
-    forward(gx)
+    for gather in (gc, gx):
+        forward(gather)
     for c in (0, 1):
         for gather in (gc, gx):
             gather.arrived(0, c)
             gather.start(3, c)
             gather.start(4, c)
-    for c in (0, 1):
-        gx.arrived(5, c)
-        gx.start(6, c)
+        if c == 0:
+            for d in (0, 1):
+                gx.arrived(5, d)
+                gx.start(6, d)
+    gk.start(1, 0)
+    gk.start(2, 1)
     gc.arrived(3, 0)
     gc.start(6, 0)
     gc.arrived(4, 1)
     gc.start(6, 1)
-    for c in (0, 1):
-        gk.start(1, c)
-        gk.start(2, c)
-    for kind, c in ((1, 1), (2, 0), (3, 0), (3, 1), (4, 0), (4, 1), (6, 0), (6, 1)):
-        gx.arrived(kind, c)
-    finished.arrived()
-    loads[4].wait()
-    gx.finish()
-    for kind, c in ((1, 1), (2, 0), (3, 1), (4, 0), (5, 0), (5, 1), (6, 0), (6, 1)):
-        gc.arrived(kind, c)
-    loads[3].wait()
 
     def normalise(buf, slot, out, which):
         cols[:, 0:8] = jnp.transpose(fin[slot])
@@ -288,37 +278,70 @@
 
         tiles(rows, body)
 
-    bsum[...] = jnp.zeros_like(bsum)
-
-    def product_h(slot):
+    finished.arrived()
+    for steps, kinds, sent in (
+        ((0, 0), (), (0, 1, 2)),
+        ((0, 1), ((2, 0),), (5,)),
+        ((0, -1), ((1, 1),), ()),
+        ((1, 0), (), (3, 4)),
+        ((1, 1), ((4, 0), (4, 1)), ()),
+        ((1, -1), ((3, 0), (3, 1)), ()),
+        ((0, 2), (), (6,)),
+        ((1, 2), ((6, 0), (6, 1)), ()),
+    ):
+        for key in kinds:
+            gx.arrived(*key)
+        for kind in sent:
+            gx.sent(kind)
+        slot = dp.slot(*steps)
         normalise(xs, slot, xs.at[slot], 0)
-
+    loads[4].wait()
+    for kind, c in ((1, 1), (2, 0), (3, 1), (4, 0), (5, 0), (5, 1), (6, 0), (6, 1)):
+        gc.arrived(kind, c)
+    loads[3].wait()
+
+    def product_h(slot, acc):
         def body(n, carry):
-            at = pl.ds(pl.multiple_of(n * MXU, MXU), MXU)
+            at = pl.ds(pl.multiple_of(n * wide, MXU), wide)
             acc[:, at] = jnp.dot(xs[slot], w[:, at], preferred_element_type=F32)
             return carry
 
-        lax.fori_loop(0, n_blocks, body, 0)
-
-    def product_g(slot):
+        lax.fori_loop(0, width // wide, body, 0)
+
+    def product_g(slot, acc):
         def body(n, carry):
-            at = pl.ds(pl.multiple_of(n * MXU, MXU), MXU)
+            at = pl.ds(pl.multiple_of(n * wide, MXU), wide)
             acc[:, at] = lax.dot_general(
                 cs[slot], w[at, :], (((1,), (1,)), ((), ())), preferred_element_type=F32
             )
             return carry
 
-        lax.fori_loop(0, n_blocks, body, 0)
-
-        def add(at):
-            c = cs[slot, at].astype(F32)
-            bsum[...] += c[0:8] + c[8:16]
-
-        tiles(rows, add)
+        lax.fori_loop(0, width // wide, body, 0)
+
+    def product_w(pair_step, ring_step, fresh=False):
+        slot = dp.slot(pair_step, ring_step)
+        normalise(ks, slot, vblk, 2)
+
+        def body(n, carry):
+            at = pl.ds(pl.multiple_of(n * wide, MXU), wide)
+            term = lax.dot_general(
+                vblk[:, at], cs[slot], (((0,), (0,)), ((), ())), preferred_element_type=F32
+            )
+            wg[at, :] = term if fresh else wg[at, :] + term
+            return carry
+
+        lax.fori_loop(0, width // wide, body, 0)
+
+    def late(i):
+        slot, to = dp.slot(*LATE[i][1:]), pl.ds(i * rows, rows)
+        return (
+            pltpu.make_async_copy(ks.at[slot], v_out.at[to], late_sem.at[2 * i]),
+            pltpu.make_async_copy(cs.at[slot], c_out.at[to], late_sem.at[2 * i + 1]),
+        )
 
     half = rows // 2
 
-    def emit(stage, start, terms):
+    def emit(stage, start, terms, acc):
         def body(i, carry):
             at = pl.ds(pl.multiple_of(start + i * TILE, TILE), TILE)
             value = acc[at]
@@ -327,7 +350,7 @@
             stage[at] = value.astype(BF16)
             return carry
 
-        lax.fori_loop(0, half // TILE, body, 0)
+        lax.fori_loop(0, half // TILE, body, 0, unroll=4)
 
     def stage_g(side, ring_step):
         place = {2: 0, 1: 1, -1: 2, 0: 3}[ring_step] * 2 + side
@@ -338,47 +361,72 @@
 
     rg = Scatter(dp, stage_g, ghalf, gleft, gright, gcross, g_ss, g_rs)
     rh = Scatter(mp, stage_h, hhalf, hleft, hright, hcross, h_ss, h_rs)
-    work = ((rg, product_g), (rh, product_h))
-
-    for side in (0, 1):
-        for scatter, product in work:
-            product(scatter.spot.slot(1 - side, 2))
-            for c in (0, 1):
-                emit(scatter.stage(side, 2), c * half, [])
-                scatter.start(0, side, c)
+    work_g, work_h = (rg, product_g), (rh, product_h)
+
+    def far(scatter, product, side):
+        product(scatter.spot.slot(1 - side, 2), acc)
+        for c in (0, 1):
+            emit(scatter.stage(side, 2), c * half, [], acc)
+            scatter.start(0, side, c)
+
+    def near(scatter, product, side):
+        product(scatter.spot.slot(1 - side, 1), acc)
+        scatter.arrived(0, side, 0)
+        for c in (0, 1):
+            emit(scatter.stage(side, 1), c * half, [] if c else [scatter.halves.at[side]], acc)
+            scatter.start(1, side, c)
+        product(scatter.spot.slot(1 - side, -1), acc)
+        for c in (0, 1):
+            if c:
+                scatter.arrived(0, side, 1)
+            emit(scatter.stage(side, -1), c * half, [scatter.halves.at[side]] if c else [], acc)
+            scatter.start(2, side, c)
+
+    def cross(scatter, c, acc):
+        scatter.arrived(1, 0, c)
+        scatter.arrived(2, 0, c)
+        emit(scatter.stage(0, 0), c * half, [scatter.left.at[0], scatter.right.at[0]], acc)
+        scatter.start(3, 0, c)
+
+    far(*work_g, 0)
+    far(*work_h, 0)
     for c in (0, 1):
         gk.start(0, c)
-    for side in (0, 1):
-        for scatter, product in work:
-            product(scatter.spot.slot(1 - side, 1))
-            emit(scatter.stage(side, 1), half, [])
-            scatter.start(1, side, 1)
-            scatter.arrived(0, side, 0)
-            emit(scatter.stage(side, 1), 0, [scatter.halves.at[side]])
-            scatter.start(1, side, 0)
-            product(scatter.spot.slot(1 - side, -1))
-            emit(scatter.stage(side, -1), 0, [])
-            scatter.start(2, side, 0)
-            scatter.arrived(0, side, 1)
-            emit(scatter.stage(side, -1), half, [scatter.halves.at[side]])
-            scatter.start(2, side, 1)
+    near(*work_g, 0)
+    near(*work_h, 0)
+    far(*work_g, 1)
+    far(*work_h, 1)
+    product_g(dp.slot(1, 0), accg)
+    cross(rg, 0, accg)
+    near(*work_g, 1)
+    near(*work_h, 1)
+    cross(rg, 1, accg)
+    product_h(mp.slot(1, 0), accg)
+    cross(rh, 0, accg)
+    cross(rh, 1, accg)
+    gk.start(1, 1)
+    gk.start(2, 0)
     forward(gk)
     for c in (0, 1):
         gk.arrived(0, c)
         gk.start(3, c)
         gk.start(4, c)
-    for scatter, product in work:
-        product(scatter.spot.slot(1, 0))
-        for c in (0, 1):
-            scatter.arrived(1, 0, c)
-            scatter.arrived(2, 0, c)
-            emit(scatter.stage(0, 0), c * half, [scatter.left.at[0], scatter.right.at[0]])
-            scatter.start(3, 0, c)
-    for c in (0, 1):
-        gk.arrived(5, c)
-        gk.start(6, c)
-
-    def whole(scatter, finish):
+
+    bsum[...] = jnp.zeros_like(bsum)
+
+    def add_block(slot, carry):
+        def add(at):
+            c = cs[slot, at].astype(F32)
+            bsum[...] += c[0:8] + c[8:16]
+
+        tiles(rows, add)
+        return carry
+
+    lax.fori_loop(0, GROUP, add_block, 0)
+    product_w(0, 0, True)
+    product_w(1, 0)
+
+    def whole(scatter, acc, finish):
         for c in (0, 1):
             for kind, side in ((1, 1), (2, 1), (3, 0)):
                 scatter.arrived(kind, side, c)
@@ -391,16 +439,6 @@
 
         tiles(rows, body)
 
-    def finish_h(at, value):
-        yout[at] = (value + bias[...]).astype(BF16)
-
-    product_h(mp.slot(0, 0))
-    whole(rh, finish_h)
-
-    product_g(dp.slot(0, 0))
-    cols[:, 0:8] = jnp.transpose(fin[dp.index])
-    colg[dp.index] = jnp.zeros(colg.shape[1:], F32)
-
     def hat_kept(at):
         return (kown[at].astype(F32) - cols[at, 2:3]) * cols[at, 3:4]
 
@@ -408,42 +446,24 @@
         hat = hat_kept(at)
         colg[dp.index, 0:1] += jnp.sum(value * hat, 0, keepdims=True)
         colg[dp.index, 1:2] += jnp.sum(value, 0, keepdims=True)
-        acc[at] = value
+        accg[at] = value
         scaled = value * gain[...]
         terms = [jnp.sum(v, 1, keepdims=True) for v in (scaled, scaled * hat)]
-        lanes = in_lanes([terms[0], terms[1]])
+        lanes = in_lanes(terms)
         cols[at, 8:16] = lanes[:, 0:8]
 
-    whole(rg, finish_g)
-    column = Spread(dp, colg, colg_ss, colg_rs)
-    column.start()
+    product_g(dp.slot(0, 0), accg)
+    product_h(mp.slot(0, 0), acc)
+    cols[:, 0:8] = jnp.transpose(fin[dp.index])
+    colg[dp.index] = jnp.zeros(colg.shape[1:], F32)
+    whole(rg, accg, finish_g)
     terms = Spread(mp, rowt, rowt_ss, rowt_rs)
     rowt[mp.index] = jnp.transpose(cols[...])[8:16]
     terms.start()
-    terms.arrived()
-    cols[:, 8:16] = jnp.transpose(terms.total() / full)
-
-    def input_grad(at):
-        hat = hat_kept(at)
-        scaled = acc[at] * gain[...]
-        grad = cols[at, 3:4] * (scaled - cols[at, 8:9] - hat * cols[at, 9:10])
-        acc[at] = grad
-
-    tiles(rows, input_grad)
+    column = Spread(dp, colg, colg_ss, colg_rs)
+    column.start()
 
     piece_rows, piece_cols = pack.shape[2:]
-
-    def packing(b, carry):
-        at = pl.ds(pl.multiple_of(b * piece_rows, piece_rows), piece_rows)
-        out = yout[at].astype(F32)
-        grad = acc[at]
-        sent = jnp.where(section == 0, out, grad)
-        yout[at] = jnp.where(section == 0, grad, out).astype(BF16)
-        for f in range(GROUP):
-            pack[b, f] = sent[:, f * piece_cols : (f + 1) * piece_cols].astype(BF16)
-        return carry
-
-    lax.fori_loop(0, GROUP, packing, 0)
     first = section == 0
     row_at = jnp.where(first, mp.index, dp.index)
     col_at = jnp.where(first, dp.index, mp.index)
@@ -464,35 +484,65 @@
         piece(i).start()
         return carry
 
-    lax.fori_loop(0, GROUP * GROUP, send_piece, 0)
+    def relay(values):
+        def packing(b, carry):
+            at = pl.ds(pl.multiple_of(b * piece_rows, piece_rows), piece_rows)
+            sent = values[at]
+            for f in range(GROUP):
+                pack[b, f] = sent[:, f * piece_cols : (f + 1) * piece_cols].astype(BF16)
+            return carry
+
+        lax.fori_loop(0, GROUP, packing, 0)
+        lax.fori_loop(0, GROUP * GROUP, send_piece, 0)
+
+    def finish_h(at, value):
+        acc[at] = value + bias[...]
+
+    whole(rh, acc, finish_h)
+
+    @pl.when(first)
+    def _():
+        relay(acc)
+
+    terms.arrived()
+    cols[:, 8:16] = jnp.transpose(terms.total() / full)
+
+    def input_grad(at):
+        hat = hat_kept(at)
+        scaled = accg[at] * gain[...]
+        accg[at] = cols[at, 3:4] * (scaled - cols[at, 8:9] - hat * cols[at, 9:10])
+
+    tiles(rows, input_grad)
+
+    @pl.when(section == 1)
+    def _():
+        relay(accg)
+
+    def keeping(at):
+        yout[at] = jnp.where(first, accg[at], acc[at]).astype(BF16)
+
+    tiles(rows, keeping)
     keep = pltpu.make_async_copy(yout, passed_out, loc_sem.at[0])
     keep.start()
 
-    wg[...] = jnp.zeros_like(wg)
-
-    def product_w(slot):
-        normalise(ks, slot, vblk, 2)
-
-        def body(n, carry):
-            at = pl.ds(pl.multiple_of(n * MXU, MXU), MXU)
-            wg[at, :] += lax.dot_general(
-                vblk[:, at], cs[slot], (((0,), (0,)), ((), ())), preferred_element_type=F32
-            )
-            return carry
-
-        lax.fori_loop(0, n_blocks, body, 0)
-
-    for kind, c in ((1, 1), (2, 0)):
-        gk.arrived(kind, c)
-    for pair_step, ring_step, kinds in (
-        (0, 0, ()), (1, 0, ()), (0, 1, ()), (0, -1, ()), (0, 2, ()), (1, 1, (4,)), (1, -1, (3,)), (1, 2, (6,))
-    ):
-        for kind in kinds:
-            for c in (0, 1):
-                gk.arrived(kind, c)
-        product_w(dp.slot(pair_step, ring_step))
+    gk.arrived(1, 1)
+    gk.arrived(2, 0)
+    product_w(0, 1)
+    product_w(0, -1)
+    for c in (0, 1):
+        gk.arrived(5, c)
+        gk.start(6, c)
+    product_w(0, 2)
     store = pltpu.make_async_copy(wg, wg_out, wg_sem)
     store.start()
+    for i in range(len(LATE)):
+        late(i)[1].start()
+    for i, (kind, pair_step, ring_step) in enumerate(LATE):
+        for c in (0, 1):
+            gk.arrived(kind, c)
+        slot = dp.slot(pair_step, ring_step)
+        normalise(ks, slot, ks.at[slot], 2)
+        late(i)[0].start()
 
     bg_out[...] = jnp.sum(bsum[...], 0, keepdims=True)
     column.arrived()
@@ -522,7 +572,32 @@
         transfer.finish()
     keep.wait()
     store.wait()
+    for i in range(len(LATE)):
+        for copy in late(i):
+            copy.wait()
     out.wait()
+
+
+def finish_kernel(
+    arrived, passed, early, late_v, late_c, bias_grad, norm_grads, next_out, passed_out, wg_out, bg_out, ng_out
+):
+    wg_out[...] = early[...] + lax.dot_general(
+        late_v[...], late_c[...], (((0,), (0,)), ((), ())), preferred_element_type=F32
+    )
+
+    @pl.when(pl.program_id(0) == 0)
+    def _():
+        piece_rows = arrived.shape[2]
+
+        def body(a, carry):
+            row = jnp.concatenate([arrived[a, e].astype(F32) for e in range(GROUP)], axis=1)
+            next_out[pl.ds(pl.multiple_of(a * piece_rows, piece_rows), piece_rows)] = row.astype(BF16)
+            return carry
+
+        lax.fori_loop(0, GROUP, body, 0)
+        passed_out[...] = passed[...]
+        bg_out[...] = bias_grad[...]
+        ng_out[...] = norm_grads[...]
 
 
 def shards(fwd_in, kept_in, cotangent, weight, bias, norm_gain, norm_shift):
@@ -535,27 +610,29 @@
     shard = pltpu.VMEM((rows, cols), BF16)
     gathered = pltpu.VMEM((GROUP, rows, cols), BF16)
     two = pltpu.VMEM((2, rows, cols), BF16)
-    arrived, passed, weight_grad, bias_grad, norm_grads = pl.pallas_call(
+    arrived, passed, early, late_v, late_c, bias_grad, norm_grads = pl.pallas_call(
         relay_kernel,
         name="relay",
         out_shape=(
             jax.ShapeDtypeStruct(piece, BF16),
             jax.ShapeDtypeStruct((rows, cols), BF16),
             jax.ShapeDtypeStruct((cols, cols), F32),
+            jax.ShapeDtypeStruct((len(LATE) * rows, cols), BF16),
+            jax.ShapeDtypeStruct((len(LATE) * rows, cols), BF16),
             jax.ShapeDtypeStruct((1, cols), F32),
             jax.ShapeDtypeStruct((2, cols), F32),
         ),
         in_specs=[any_spec] * 4 + [vmem_spec] * 3,
-        out_specs=(any_spec, any_spec, any_spec, vmem_spec, vmem_spec),
+        out_specs=(any_spec,) * 5 + (vmem_spec,) * 2,
         scratch_shapes=[
             gathered, gathered, gathered, pltpu.VMEM((cols, cols), BF16), shard, pltpu.VMEM((cols, cols), F32),
             pltpu.VMEM((7, rows, cols), BF16),
             two, two, two, shard, two, two, two, shard,
-            shard, pltpu.VMEM((rows, cols), F32), shard, pltpu.VMEM((rows, 128), F32),
+            shard, pltpu.VMEM((rows, cols), F32), pltpu.VMEM((rows, cols), F32), shard, pltpu.VMEM((rows, 128), F32),
             pltpu.VMEM((GROUP, 8, rows), F32), pltpu.VMEM((GROUP, 8, rows), F32), pltpu.VMEM((GROUP, 8, rows), F32),
             pltpu.VMEM((GROUP, 2, cols), F32), pltpu.VMEM((8, cols), F32),
             pltpu.VMEM(piece, BF16), pltpu.VMEM(piece, BF16),
-            dma((5,)), dma,
+            dma((5,)), dma, dma((2 * len(LATE),)),
             dma((7, 2)), dma((7, 2)), dma((7, 2)), dma((7, 2)), dma((7, 2)), dma((7, 2)),
             dma((16,)), dma((16,)), dma((16,)), dma((16,)),
             dma((7,)), dma((7,)), dma((7,)), dma((7,)), dma((7,)), dma((7,)), dma((7,)), dma((7,)),
@@ -573,9 +650,33 @@
         norm_gain.reshape(1, cols),
         norm_shift.reshape(1, cols),
     )
-    next_in = arrived.transpose(0, 2, 1, 3).reshape(fwd_in.shape)
+    fixed = lambda *shape: pl.BlockSpec(shape, lambda i: (0,) * len(shape))
+    tile = pl.BlockSpec((MXU, cols), lambda i: (i, 0))
+    next_in, passed, weight_grad, bias_grad, norm_grads = pl.pallas_call(
+        finish_kernel,
+        name="finish",
+        grid=(cols // MXU,),
+        out_shape=(
+            jax.ShapeDtypeStruct((rows, cols), BF16),
+            jax.ShapeDtypeStruct((rows, cols), BF16),
+            jax.ShapeDtypeStruct((cols, cols), F32),
+            jax.ShapeDtypeStruct((1, cols), F32),
+            jax.ShapeDtypeStruct((2, cols), F32),
+        ),
+        in_specs=[
+            fixed(*piece),
+            fixed(rows, cols),
+            tile,
+            pl.BlockSpec((len(LATE) * rows, MXU), lambda i: (0, i)),
+            fixed(len(LATE) * rows, cols),
+            fixed(1, cols),
+            fixed(2, cols),
+        ],
+        out_specs=(fixed(rows, cols), fixed(rows, cols), tile, fixed(1, cols), fixed(2, cols)),
+        compiler_params=pltpu.CompilerParams(vmem_limit_bytes=60 * 2**20),
+    )(arrived, passed, early, late_v, late_c, bias_grad, norm_grads)
     return (
-        next_in,
+        next_in.reshape(fwd_in.shape),
         passed.reshape(fwd_in.shape),
         weight_grad.reshape(1, cols, cols),
         bias_grad,

time: 243 us -> 186 us (0.77)
  Pallas kernels: 227 us -> 185 us
  local copies, waits for them, and re-layouts: 15.2 us -> 0 us
    pallas_call x1, Pallas kernels: 227 us -> 171 us  [shards(): pl.pallas_call(relay_kernel, name='relay', out_shape=(jax.ShapeDtypeStruc...]
    pallas_call x0 -> x1, Pallas kernels: none -> 13.8 us  [shards(): pl.pallas_call(finish_kernel, name='finish', grid=(cols // MXU,), out_sha...]
    unnamed x8 -> x0, local copies, waits for them, and re-layouts: 11.6 us -> none
where the time goes in v2:
time: 186 us
  Pallas kernels  185 us (99%)
    pallas_call x1, Pallas kernels, shards(): pl.pallas_call(relay_kernel, name='relay', out_shape=(jax.ShapeDtypeStruc...  171 us
    pallas_call x1, Pallas kernels, shards(): pl.pallas_call(finish_kernel, name='finish', grid=(cols // MXU,), out_sha...  13.8 us

profile of v2, /device:TPU:0, one launch (start us, length us, event | category | flops | bytes accessed | tf_op | source)
XLA Modules:
  0.0 185.5 jit_solution(3913468983734600297)
XLA Ops:
  0.6 170.9 %relay.1 = (bf16[8,8,32,192]{3,2,1,0:T(8,128)(2,1)}, bf16[256,1536]{1,0:T(8,128)(2,1)}, f32[1536,1536]{1,0:T(8,128)}, bf16[768,1536]{1,0:T(8,128)(2,1)}, bf16[76...) custom-call(bf16[256,1536]{1,0:T(8,128)(2,1)} %bitcast.9, bf16[256,1536]{1,0:T(8,128)(2,1)} %bitcast.10, ...), custom_call_target="tpu_custom_call" | custom-call | tf_op jit(solution)/shard_map/relay/pallas_call | solution.py:613
  171.6 13.8 %finish.1 = (bf16[256,1536]{1,0:T(8,128)(2,1)}, bf16[256,1536]{1,0:T(8,128)(2,1)}, f32[1536,1536]{1,0:T(8,128)}, f32[1,1536]{1,0:T(1,128)}, f32[2,1536]{1,0:T(2,128)}) custom-call(bf16[8,8,32,192]{3,2,1,0:T(8,128)(2,1)} %get-tuple-element.17.arrived, bf16[256,1536]{1,0:T(8,128)(2,1)} %get-tuple-element.18.passed, f32[1536,1536]{1,0:T(8,128)} %get-tuple-element.19.early, ...), custom_call_target="tpu_custom_call" | custom-call | tf_op jit(solution)/shard_map/finish/pallas_call | solution.py:655

commit v3 on v2

--- a/solution.py
+++ b/solution.py
@@ -10,8 +10,8 @@
 PAIR = 2
 GROUP = RING * PAIR
 TILE = 16
-LATE = ((4, 1, 1), (3, 1, -1), (6, 1, 2))
 MXU = 256
+LANES = 128
 F32 = jnp.float32
 BF16 = jnp.bfloat16
 MESH = pl.DeviceIdType.MESH
@@ -33,14 +33,14 @@
 
 
 class Gather:
-    def __init__(self, spot, buf, send_sem, recv_sem, far_by_pair):
-        self.spot, self.buf, self.far_by_pair = spot, buf, far_by_pair
+    def __init__(self, spot, buf, send_sem, recv_sem, far_by_pair, parts=2):
+        self.spot, self.buf, self.far_by_pair, self.parts = spot, buf, far_by_pair, parts
         self.send_sem, self.recv_sem = send_sem, recv_sem
-        self.half = buf.shape[1] // 2
+        self.part = buf.shape[1] // parts
         self.started = []
 
     def route(self, kind, c):
-        step = 1 if c == 0 else -1
+        step = 1 if c < self.parts // 2 else -1
         return {
             0: ((0, 0), (1, 0), (1, 0)),
             1: ((0, 0), (0, 1), (0, -1)),
@@ -48,13 +48,15 @@
             3: ((1, 0), (0, 1), (1, -1)),
             4: ((1, 0), (0, -1), (1, 1)),
             5: ((0, -step), (0, step), (0, 2)),
+            7: ((0, -1), (1, 0), (1, -1)),
+            8: ((0, 1), (1, 0), (1, 1)),
             6: ((0, 2), (1, 0), (1, 2)) if self.far_by_pair else ((1, -step), (0, step), (1, 2)),
         }[kind]
 
     def copy(self, kind, c, landing):
         source, target, lands = self.route(kind, c)
         here = self.spot.slot(*(lands if landing else source))
-        view = self.buf.at[here, pl.ds(c * self.half, self.half)]
+        view = self.buf.at[here, pl.ds(c * self.part, self.part)]
         return pltpu.make_async_remote_copy(
             src_ref=view,
             dst_ref=view,
@@ -158,6 +160,14 @@
         return result
 
 
+def swap_halves(first, second):
+    left = lax.broadcasted_iota(jnp.int32, first.shape, 1) < LANES // 2
+    return (
+        jnp.where(left, first, pltpu.roll(second, LANES // 2, 1)),
+        jnp.where(left, pltpu.roll(first, LANES // 2, 1), second),
+    )
+
+
 def tiles(count, body, size=TILE):
     def step(i, carry):
         body(pl.ds(pl.multiple_of(i * size, size), size))
@@ -168,10 +178,10 @@
 
 def relay_kernel(
     fwd, kept, cot, weight, bias, gain, shift,
-    arrived_out, passed_out, wg_out, v_out, c_out, bg_out, ng_out,
+    arrived_out, passed_out, wg_out, bg_out, ng_out,
     xs, ks, cs, w, kown, wg, gst, hhalf, hleft, hright, hcross, ghalf, gleft, gright, gcross,
     vblk, acc, accg, yout, cols, stat, fin, rowt, colg, bsum, pack, land,
-    loc_sem, wg_sem, late_sem,
+    loc_sem, wg_sem,
     c_ss, c_rs, x_ss, x_rs, k_ss, k_rs, h_ss, h_rs, g_ss, g_rs,
     stat_ss, stat_rs, fin_ss, fin_rs, rowt_ss, rowt_rs, colg_ss, colg_rs, a_ss, a_rs,
 ):
@@ -223,7 +233,7 @@
 
     gc = Gather(mp, cs, c_ss, c_rs, False)
     gx = Gather(dp, xs, x_ss, x_rs, True)
-    gk = Gather(dp, ks, k_ss, k_rs, True)
+    gk = Gather(dp, ks, k_ss, k_rs, True, 4)
     stats = Spread(mp, stat, stat_ss, stat_rs)
     stats.start()
     for c in (0, 1):
@@ -260,8 +270,9 @@
             for d in (0, 1):
                 gx.arrived(5, d)
                 gx.start(6, d)
-    gk.start(1, 0)
-    gk.start(2, 1)
+    for c in range(3):
+        gk.start(1, c)
+        gk.start(2, 3 - c)
     gc.arrived(3, 0)
     gc.start(6, 0)
     gc.arrived(4, 1)
@@ -332,13 +343,6 @@
 
         lax.fori_loop(0, width // wide, body, 0)
 
-    def late(i):
-        slot, to = dp.slot(*LATE[i][1:]), pl.ds(i * rows, rows)
-        return (
-            pltpu.make_async_copy(ks.at[slot], v_out.at[to], late_sem.at[2 * i]),
-            pltpu.make_async_copy(cs.at[slot], c_out.at[to], late_sem.at[2 * i + 1]),
-        )
-
     half = rows // 2
 
     def emit(stage, start, terms, acc):
@@ -390,12 +394,21 @@
 
     far(*work_g, 0)
     far(*work_h, 0)
-    for c in (0, 1):
+    for c in range(4):
         gk.start(0, c)
+    for kind, c in ((1, 0), (2, 3)):
+        gk.arrived(kind, c)
+        gk.start(kind + 6, c)
     near(*work_g, 0)
     near(*work_h, 0)
     far(*work_g, 1)
     far(*work_h, 1)
+    gk.start(5, 0)
+    gk.start(5, 3)
+    gk.arrived(1, 1)
+    gk.start(5, 1)
+    gk.arrived(2, 2)
+    gk.start(5, 2)
     product_g(dp.slot(1, 0), accg)
     cross(rg, 0, accg)
     near(*work_g, 1)
@@ -404,13 +417,17 @@
     product_h(mp.slot(1, 0), accg)
     cross(rh, 0, accg)
     cross(rh, 1, accg)
-    gk.start(1, 1)
+    gk.start(1, 3)
     gk.start(2, 0)
-    forward(gk)
-    for c in (0, 1):
+    for c in range(4):
         gk.arrived(0, c)
-        gk.start(3, c)
-        gk.start(4, c)
+        if c != 0:
+            gk.start(3, c)
+        if c != 3:
+            gk.start(4, c)
+    for c in range(4):
+        gk.arrived(5, c)
+        gk.start(6, c)
 
     bsum[...] = jnp.zeros_like(bsum)
 
@@ -425,6 +442,7 @@
     lax.fori_loop(0, GROUP, add_block, 0)
     product_w(0, 0, True)
     product_w(1, 0)
+    product_w(0, 2)
 
     def whole(scatter, acc, finish):
         for c in (0, 1):
@@ -463,7 +481,7 @@
     column = Spread(dp, colg, colg_ss, colg_rs)
     column.start()
 
-    piece_rows, piece_cols = pack.shape[2:]
+    piece_rows = rows // GROUP
     first = section == 0
     row_at = jnp.where(first, mp.index, dp.index)
     col_at = jnp.where(first, dp.index, mp.index)
@@ -474,8 +492,8 @@
         return pltpu.make_async_remote_copy(
             src_ref=pack.at[b, f],
             dst_ref=land.at[row_at, col_at],
-            send_sem=a_ss.at[j],
-            recv_sem=a_rs.at[row_at * GROUP + col_at],
+            send_sem=a_ss,
+            recv_sem=a_rs,
             device_id={"section": 1 - section, "dp": jnp.where(first, b, f), "mp": jnp.where(first, f, b)},
             device_id_type=MESH,
         )
@@ -483,13 +501,28 @@
     def send_piece(i, carry):
         piece(i).start()
         return carry
+
+    odd = lax.rem(col_at, 2) == 1
+    low = lax.broadcasted_iota(jnp.int32, (piece_rows, LANES), 1) < LANES // 2
+
+    def halves(value):
+        return value[: piece_rows // 2], value[piece_rows // 2 :]
 
     def relay(values):
         def packing(b, carry):
             at = pl.ds(pl.multiple_of(b * piece_rows, piece_rows), piece_rows)
             sent = values[at]
-            for f in range(GROUP):
-                pack[b, f] = sent[:, f * piece_cols : (f + 1) * piece_cols].astype(BF16)
+            for k in range(GROUP // 2):
+                left, shared, right = (sent[:, (3 * k + i) * LANES : (3 * k + i + 1) * LANES] for i in range(3))
+                turned = [pltpu.roll(v, LANES // 2, 1) for v in (left, shared, right)]
+                early = jnp.where(odd, jnp.where(low, turned[0], turned[1]), left)
+                later = jnp.where(odd, right, jnp.where(low, turned[1], turned[2]))
+                early_half = swap_halves(*halves(jnp.where(odd, left, shared)))[0]
+                later_half = swap_halves(*halves(jnp.where(odd, shared, right)))[1]
+                pack[b, 2 * k, 0:piece_rows] = early.astype(BF16)
+                pack[b, 2 * k + 1, 0:piece_rows] = later.astype(BF16)
+                pack[b, 2 * k, piece_rows:] = early_half.astype(BF16)
+                pack[b, 2 * k + 1, piece_rows:] = later_half.astype(BF16)
             return carry
 
         lax.fori_loop(0, GROUP, packing, 0)
@@ -525,73 +558,75 @@
     keep = pltpu.make_async_copy(yout, passed_out, loc_sem.at[0])
     keep.start()
 
-    gk.arrived(1, 1)
-    gk.arrived(2, 0)
-    product_w(0, 1)
-    product_w(0, -1)
-    for c in (0, 1):
-        gk.arrived(5, c)
-        gk.start(6, c)
-    product_w(0, 2)
-    store = pltpu.make_async_copy(wg, wg_out, wg_sem)
-    store.start()
-    for i in range(len(LATE)):
-        late(i)[1].start()
-    for i, (kind, pair_step, ring_step) in enumerate(LATE):
-        for c in (0, 1):
-            gk.arrived(kind, c)
-        slot = dp.slot(pair_step, ring_step)
-        normalise(ks, slot, ks.at[slot], 2)
-        late(i)[0].start()
+    for steps, kinds in (
+        ((0, 1), ((2, 1), (2, 0))),
+        ((0, -1), ((1, 2), (1, 3))),
+        ((1, 1), ((4, 0), (4, 1), (4, 2), (8, 3))),
+        ((1, -1), ((3, 1), (3, 2), (3, 3), (7, 0))),
+    ):
+        for key in kinds:
+            gk.arrived(*key)
+        product_w(*steps)
+    every_piece = pltpu.make_async_remote_copy(
+        src_ref=pack,
+        dst_ref=land,
+        send_sem=a_ss,
+        recv_sem=a_rs,
+        device_id={"section": 1 - section},
+        device_id_type=MESH,
+    )
+    every_piece.wait_recv()
+    out = pltpu.make_async_copy(land, arrived_out, loc_sem.at[1])
+    out.start()
+    for c in range(4):
+        gk.arrived(6, c)
+    rh.finish()
+    slot = dp.slot(1, 2)
+    normalise(ks, slot, vblk, 2)
+
+    def store(n):
+        at = pl.ds(pl.multiple_of(n * rows, rows), rows)
+        return pltpu.make_async_copy(xs.at[n], wg_out.at[at], wg_sem.at[n])
+
+    def last(n, carry):
+        at = pl.ds(pl.multiple_of(n * rows, rows), rows)
+        term = lax.dot_general(vblk[:, at], cs[slot], (((0,), (0,)), ((), ())), preferred_element_type=F32)
+        xs[n] = (wg[at, :] + term).astype(BF16)
+        store(n).start()
+        return carry
+
+    lax.fori_loop(0, width // rows, last, 0)
 
     bg_out[...] = jnp.sum(bsum[...], 0, keepdims=True)
     column.arrived()
     ng_out[...] = column.total()
 
-    def landed(i, carry):
-        pltpu.make_async_remote_copy(
-            src_ref=pack.at[0, 0],
-            dst_ref=land.at[lax.div(i, GROUP), lax.rem(i, GROUP)],
-            send_sem=a_ss.at[i],
-            recv_sem=a_rs.at[i],
-            device_id={"section": 1 - section},
-            device_id_type=MESH,
-        ).wait_recv()
-        return carry
-
-    lax.fori_loop(0, GROUP * GROUP, landed, 0)
-    out = pltpu.make_async_copy(land, arrived_out, loc_sem.at[1])
-    out.start()
-
-    def left(i, carry):
-        piece(i).wait_send()
-        return carry
-
-    lax.fori_loop(0, GROUP * GROUP, left, 0)
+    every_piece.wait_send()
     for transfer in (gc, gk, rg, rh, stats, finished, column, terms):
         transfer.finish()
     keep.wait()
-    store.wait()
-    for i in range(len(LATE)):
-        for copy in late(i):
-            copy.wait()
+    for n in range(width // rows):
+        store(n).wait()
     out.wait()
 
 
 def finish_kernel(
-    arrived, passed, early, late_v, late_c, bias_grad, norm_grads, next_out, passed_out, wg_out, bg_out, ng_out
+    arrived, passed, grad, bias_grad, norm_grads, next_out, passed_out, wg_out, bg_out, ng_out
 ):
-    wg_out[...] = early[...] + lax.dot_general(
-        late_v[...], late_c[...], (((0,), (0,)), ((), ())), preferred_element_type=F32
-    )
+    wg_out[...] = grad[...].astype(F32)
 
     @pl.when(pl.program_id(0) == 0)
     def _():
-        piece_rows = arrived.shape[2]
+        piece_rows = next_out.shape[0] // GROUP
 
         def body(a, carry):
-            row = jnp.concatenate([arrived[a, e].astype(F32) for e in range(GROUP)], axis=1)
-            next_out[pl.ds(pl.multiple_of(a * piece_rows, piece_rows), piece_rows)] = row.astype(BF16)
+            at = pl.ds(pl.multiple_of(a * piece_rows, piece_rows), piece_rows)
+            for k in range(GROUP // 2):
+                even, odd = arrived[a, 2 * k], arrived[a, 2 * k + 1]
+                shared = swap_halves(even[piece_rows:].astype(F32), odd[piece_rows:].astype(F32))
+                columns = (even[:piece_rows], jnp.concatenate(shared, axis=0).astype(BF16), odd[:piece_rows])
+                for i, column in enumerate(columns):
+                    next_out[at, (3 * k + i) * LANES : (3 * k + i + 1) * LANES] = column
             return carry
 
         lax.fori_loop(0, GROUP, body, 0)
@@ -603,27 +638,25 @@
 def shards(fwd_in, kept_in, cotangent, weight, bias, norm_gain, norm_shift):
     section_index = lax.axis_index("section")
     rows, cols = fwd_in.shape[3:]
-    piece = (GROUP, GROUP, rows // GROUP, cols // GROUP)
+    piece = (GROUP, GROUP, rows // GROUP * 3 // 2, LANES)
     any_spec = pl.BlockSpec(memory_space=pl.ANY)
     vmem_spec = pl.BlockSpec(memory_space=pltpu.VMEM)
     dma = pltpu.SemaphoreType.DMA
     shard = pltpu.VMEM((rows, cols), BF16)
     gathered = pltpu.VMEM((GROUP, rows, cols), BF16)
     two = pltpu.VMEM((2, rows, cols), BF16)
-    arrived, passed, early, late_v, late_c, bias_grad, norm_grads = pl.pallas_call(
+    arrived, passed, grad, bias_grad, norm_grads = pl.pallas_call(
         relay_kernel,
         name="relay",
         out_shape=(
             jax.ShapeDtypeStruct(piece, BF16),
             jax.ShapeDtypeStruct((rows, cols), BF16),
-            jax.ShapeDtypeStruct((cols, cols), F32),
-            jax.ShapeDtypeStruct((len(LATE) * rows, cols), BF16),
-            jax.ShapeDtypeStruct((len(LATE) * rows, cols), BF16),
+            jax.ShapeDtypeStruct((cols, cols), BF16),
             jax.ShapeDtypeStruct((1, cols), F32),
             jax.ShapeDtypeStruct((2, cols), F32),
         ),
         in_specs=[any_spec] * 4 + [vmem_spec] * 3,
-        out_specs=(any_spec,) * 5 + (vmem_spec,) * 2,
+        out_specs=(any_spec,) * 3 + (vmem_spec,) * 2,
         scratch_shapes=[
             gathered, gathered, gathered, pltpu.VMEM((cols, cols), BF16), shard, pltpu.VMEM((cols, cols), F32),
             pltpu.VMEM((7, rows, cols), BF16),
@@ -632,11 +665,11 @@
             pltpu.VMEM((GROUP, 8, rows), F32), pltpu.VMEM((GROUP, 8, rows), F32), pltpu.VMEM((GROUP, 8, rows), F32),
             pltpu.VMEM((GROUP, 2, cols), F32), pltpu.VMEM((8, cols), F32),
             pltpu.VMEM(piece, BF16), pltpu.VMEM(piece, BF16),
-            dma((5,)), dma, dma((2 * len(LATE),)),
-            dma((7, 2)), dma((7, 2)), dma((7, 2)), dma((7, 2)), dma((7, 2)), dma((7, 2)),
+            dma((5,)), dma((cols // rows,)),
+            dma((7, 2)), dma((7, 2)), dma((7, 2)), dma((7, 2)), dma((9, 4)), dma((9, 4)),
             dma((16,)), dma((16,)), dma((16,)), dma((16,)),
             dma((7,)), dma((7,)), dma((7,)), dma((7,)), dma((7,)), dma((7,)), dma((7,)), dma((7,)),
-            dma((GROUP * GROUP,)), dma((GROUP * GROUP,)),
+            dma, dma,
         ],
         compiler_params=pltpu.CompilerParams(
             collective_id=0, has_side_effects=True, vmem_limit_bytes=60 * 2**20
@@ -667,14 +700,12 @@
             fixed(*piece),
             fixed(rows, cols),
             tile,
-            pl.BlockSpec((len(LATE) * rows, MXU), lambda i: (0, i)),
-            fixed(len(LATE) * rows, cols),
             fixed(1, cols),
             fixed(2, cols),
         ],
         out_specs=(fixed(rows, cols), fixed(rows, cols), tile, fixed(1, cols), fixed(2, cols)),
         compiler_params=pltpu.CompilerParams(vmem_limit_bytes=60 * 2**20),
-    )(arrived, passed, early, late_v, late_c, bias_grad, norm_grads)
+    )(arrived, passed, grad, bias_grad, norm_grads)
     return (
         next_in.reshape(fwd_in.shape),
         passed.reshape(fwd_in.shape),

time: 186 us -> 179 us (0.962)
  Pallas kernels: 185 us -> 178 us
    pallas_call x1, Pallas kernels: 13.8 us -> 8.6 us  [shards(): pl.pallas_call(finish_kernel, name='finish', grid=(cols // MXU,), out_sha...]
where the time goes in v3:
time: 179 us
  Pallas kernels  178 us (99%)
    pallas_call x1, Pallas kernels, shards(): pl.pallas_call(relay_kernel, name='relay', out_shape=(jax.ShapeDtypeStruc...  169 us
    pallas_call x1, Pallas kernels, shards(): pl.pallas_call(finish_kernel, name='finish', grid=(cols // MXU,), out_sha...  8.6 us

profile of v3, /device:TPU:0, one launch (start us, length us, event | category | flops | bytes accessed | tf_op | source)
XLA Modules:
  0.0 178.6 jit_solution(9434393772567711517)
XLA Ops:
  0.6 169.4 %relay.1 = (bf16[8,8,48,128]{3,2,1,0:T(8,128)(2,1)}, bf16[256,1536]{1,0:T(8,128)(2,1)}, bf16[1536,1536]{1,0:T(8,128)(2,1)}, f32[1,1536]{1,0:T(1,128)}, f32[2,1536]{1,0:T(2,128)}) custom-call(bf16[256,1536]{1,0:T(8,128)(2,1)} %bitcast.9, bf16[256,1536]{1,0:T(8,128)(2,1)} %bitcast.10, bf16[256,1536]{1,0:T(8,128)(2,1)} %bitcast.11, bf16[1536,1536]{1,0:T(8,128)(2,1)} %bitcast.8, ...), custom_call_target="tpu_custom_call" | custom-call | tf_op jit(solution)/shard_map/relay/pallas_call | solution.py:648
  170.0 8.6 %finish.1 = (bf16[256,1536]{1,0:T(8,128)(2,1)}, bf16[256,1536]{1,0:T(8,128)(2,1)}, f32[1536,1536]{1,0:T(8,128)}, f32[1,1536]{1,0:T(1,128)}, f32[2,1536]{1,0:T(2,128)}) custom-call(bf16[8,8,48,128]{3,2,1,0:T(8,128)(2,1)} %get-tuple-element.15.arrived, bf16[256,1536]{1,0:T(8,128)(2,1)} %get-tuple-element.16.passed, bf16[1536,1536]{1,0:T(8,128)(2,1)} %get-tuple-element.17.grad, ...), custom_call_target="tpu_custom_call" | custom-call | tf_op jit(solution)/shard_map/finish/pallas_call | solution.py:688

commit v4 on v3

--- a/solution.py
+++ b/solution.py
@@ -49,6 +49,7 @@
             4: ((1, 0), (0, -1), (1, 1)),
             5: ((0, -step), (0, step), (0, 2)),
             7: ((0, -1), (1, 0), (1, -1)),
+            9: ((1, -step), (0, step), (1, 2)),
             8: ((0, 1), (1, 0), (1, 1)),
             6: ((0, 2), (1, 0), (1, 2)) if self.far_by_pair else ((1, -step), (0, step), (1, 2)),
         }[kind]
@@ -273,6 +274,8 @@
     for c in range(3):
         gk.start(1, c)
         gk.start(2, 3 - c)
+    for c in range(4):
+        gk.start(0, c)
     gc.arrived(3, 0)
     gc.start(6, 0)
     gc.arrived(4, 1)
@@ -394,8 +397,6 @@
 
     far(*work_g, 0)
     far(*work_h, 0)
-    for c in range(4):
-        gk.start(0, c)
     for kind, c in ((1, 0), (2, 3)):
         gk.arrived(kind, c)
         gk.start(kind + 6, c)
@@ -403,6 +404,8 @@
     near(*work_h, 0)
     far(*work_g, 1)
     far(*work_h, 1)
+    gk.start(1, 3)
+    gk.start(2, 0)
     gk.start(5, 0)
     gk.start(5, 3)
     gk.arrived(1, 1)
@@ -417,8 +420,6 @@
     product_h(mp.slot(1, 0), accg)
     cross(rh, 0, accg)
     cross(rh, 1, accg)
-    gk.start(1, 3)
-    gk.start(2, 0)
     for c in range(4):
         gk.arrived(0, c)
         if c != 0:
@@ -427,7 +428,11 @@
             gk.start(4, c)
     for c in range(4):
         gk.arrived(5, c)
-        gk.start(6, c)
+        if c in (1, 2):
+            gk.start(6, c)
+    for kind, c in ((7, 0), (8, 3)):
+        gk.arrived(kind, c)
+        gk.start(9, c)
 
     bsum[...] = jnp.zeros_like(bsum)
 
@@ -443,6 +448,10 @@
     product_w(0, 0, True)
     product_w(1, 0)
     product_w(0, 2)
+    for kind, c in ((2, 1), (2, 0), (1, 2), (1, 3)):
+        gk.arrived(kind, c)
+    product_w(0, 1)
+    product_w(0, -1)
 
     def whole(scatter, acc, finish):
         for c in (0, 1):
@@ -559,10 +568,8 @@
     keep.start()
 
     for steps, kinds in (
-        ((0, 1), ((2, 1), (2, 0))),
-        ((0, -1), ((1, 2), (1, 3))),
-        ((1, 1), ((4, 0), (4, 1), (4, 2), (8, 3))),
-        ((1, -1), ((3, 1), (3, 2), (3, 3), (7, 0))),
+        ((1, 1), ((4, 0), (4, 1), (4, 2))),
+        ((1, -1), ((3, 1), (3, 2), (3, 3))),
     ):
         for key in kinds:
             gk.arrived(*key)
@@ -578,8 +585,8 @@
     every_piece.wait_recv()
     out = pltpu.make_async_copy(land, arrived_out, loc_sem.at[1])
     out.start()
-    for c in range(4):
-        gk.arrived(6, c)
+    for key in ((6, 1), (6, 2), (9, 0), (9, 3)):
+        gk.arrived(*key)
     rh.finish()
     slot = dp.slot(1, 2)
     normalise(ks, slot, vblk, 2)
@@ -666,7 +673,7 @@
             pltpu.VMEM((GROUP, 2, cols), F32), pltpu.VMEM((8, cols), F32),
             pltpu.VMEM(piece, BF16), pltpu.VMEM(piece, BF16),
             dma((5,)), dma((cols // rows,)),
-            dma((7, 2)), dma((7, 2)), dma((7, 2)), dma((7, 2)), dma((9, 4)), dma((9, 4)),
+            dma((7, 2)), dma((7, 2)), dma((7, 2)), dma((7, 2)), dma((10, 4)), dma((10, 4)),
             dma((16,)), dma((16,)), dma((16,)), dma((16,)),
             dma((7,)), dma((7,)), dma((7,)), dma((7,)), dma((7,)), dma((7,)), dma((7,)), dma((7,)),
             dma, dma,

time: 179 us -> 176 us (0.983)
  Pallas kernels: 178 us -> 174 us
    pallas_call x1, Pallas kernels: 169 us -> 165 us  [shards(): pl.pallas_call(relay_kernel, name='relay', out_shape=(jax.ShapeDtypeStruc...]
where the time goes in v4:
time: 176 us; the launch traced here: 174 us
  Pallas kernels  174 us (99%)
    pallas_call x1, Pallas kernels, shards(): pl.pallas_call(relay_kernel, name='relay', out_shape=(jax.ShapeDtypeStruc...  165 us
    pallas_call x1, Pallas kernels, shards(): pl.pallas_call(finish_kernel, name='finish', grid=(cols // MXU,), out_sha...  8.6 us

profile of v4, /device:TPU:0, one launch (start us, length us, event | category | flops | bytes accessed | tf_op | source)
XLA Modules:
  0.0 174.3 jit_solution(12949116594812545172)
XLA Ops:
  0.6 165.1 %relay.1 = (bf16[8,8,48,128]{3,2,1,0:T(8,128)(2,1)}, bf16[256,1536]{1,0:T(8,128)(2,1)}, bf16[1536,1536]{1,0:T(8,128)(2,1)}, f32[1,1536]{1,0:T(1,128)}, f32[2,1536]{1,0:T(2,128)}) custom-call(bf16[256,1536]{1,0:T(8,128)(2,1)} %bitcast.9, bf16[256,1536]{1,0:T(8,128)(2,1)} %bitcast.10, bf16[256,1536]{1,0:T(8,128)(2,1)} %bitcast.11, bf16[1536,1536]{1,0:T(8,128)(2,1)} %bitcast.8, ...), custom_call_target="tpu_custom_call" | custom-call | tf_op jit(solution)/shard_map/relay/pallas_call | solution.py:655
  165.7 8.6 %finish.1 = (bf16[256,1536]{1,0:T(8,128)(2,1)}, bf16[256,1536]{1,0:T(8,128)(2,1)}, f32[1536,1536]{1,0:T(8,128)}, f32[1,1536]{1,0:T(1,128)}, f32[2,1536]{1,0:T(2,128)}) custom-call(bf16[8,8,48,128]{3,2,1,0:T(8,128)(2,1)} %get-tuple-element.15.arrived, bf16[256,1536]{1,0:T(8,128)(2,1)} %get-tuple-element.16.passed, bf16[1536,1536]{1,0:T(8,128)(2,1)} %get-tuple-element.17.grad, ...), custom_call_target="tpu_custom_call" | custom-call | tf_op jit(solution)/shard_map/finish/pallas_call | solution.py:695

commit v5 on v4

--- a/solution.py
+++ b/solution.py
@@ -582,9 +582,6 @@
         device_id={"section": 1 - section},
         device_id_type=MESH,
     )
-    every_piece.wait_recv()
-    out = pltpu.make_async_copy(land, arrived_out, loc_sem.at[1])
-    out.start()
     for key in ((6, 1), (6, 2), (9, 0), (9, 3)):
         gk.arrived(*key)
     rh.finish()
@@ -603,6 +600,9 @@
         return carry
 
     lax.fori_loop(0, width // rows, last, 0)
+    every_piece.wait_recv()
+    out = pltpu.make_async_copy(land, arrived_out, loc_sem.at[1])
+    out.start()
 
     bg_out[...] = jnp.sum(bsum[...], 0, keepdims=True)
     column.arrived()

time: 176 us -> 176 us (level)
  no operation moved by 1% of the time
where the time goes in v5:
time: 176 us; the launch traced here: 175 us
  Pallas kernels  174 us (99%)
    pallas_call x1, Pallas kernels, shards(): pl.pallas_call(relay_kernel, name='relay', out_shape=(jax.ShapeDtypeStruc...  165 us
    pallas_call x1, Pallas kernels, shards(): pl.pallas_call(finish_kernel, name='finish', grid=(cols // MXU,), out_sha...  8.6 us

profile of v5, /device:TPU:0, one launch (start us, length us, event | category | flops | bytes accessed | tf_op | source)
XLA Modules:
  0.0 174.6 jit_solution(4732159700568109300)
XLA Ops:
  0.6 165.4 %relay.1 = (bf16[8,8,48,128]{3,2,1,0:T(8,128)(2,1)}, bf16[256,1536]{1,0:T(8,128)(2,1)}, bf16[1536,1536]{1,0:T(8,128)(2,1)}, f32[1,1536]{1,0:T(1,128)}, f32[2,1536]{1,0:T(2,128)}) custom-call(bf16[256,1536]{1,0:T(8,128)(2,1)} %bitcast.9, bf16[256,1536]{1,0:T(8,128)(2,1)} %bitcast.10, bf16[256,1536]{1,0:T(8,128)(2,1)} %bitcast.11, bf16[1536,1536]{1,0:T(8,128)(2,1)} %bitcast.8, ...), custom_call_target="tpu_custom_call" | custom-call | tf_op jit(solution)/shard_map/relay/pallas_call | solution.py:655
  166.0 8.6 %finish.1 = (bf16[256,1536]{1,0:T(8,128)(2,1)}, bf16[256,1536]{1,0:T(8,128)(2,1)}, f32[1536,1536]{1,0:T(8,128)}, f32[1,1536]{1,0:T(1,128)}, f32[2,1536]{1,0:T(2,128)}) custom-call(bf16[8,8,48,128]{3,2,1,0:T(8,128)(2,1)} %get-tuple-element.15.arrived, bf16[256,1536]{1,0:T(8,128)(2,1)} %get-tuple-element.16.passed, bf16[1536,1536]{1,0:T(8,128)(2,1)} %get-tuple-element.17.grad, ...), custom_call_target="tpu_custom_call" | custom-call | tf_op jit(solution)/shard_map/finish/pallas_call | solution.py:695
